TPU v7x, 256 devices: a whole 4x4x8 slice. The times are simulated.
256 devices in a mesh: role: 2 (over core), gx: 16 (over z, y_hi), gy: 8 (over x, y_lo).
Axes of the slice: x: 4, y: 4 (y_hi: 2, y_lo: 2; y = y_hi * 2 + y_lo), z: 8, core: 2. Of those that a mesh axis runs over, the one named last changes fastest.
Arguments:
- velocity: float32 [3, 384, 384, 128], P(None, 'gx', ('role', 'gy')), may hold values from -5 to 5
- target_field: float32 [3, 384, 384, 128], P(None, 'gx', ('role', 'gy')), may hold values from -4 to 4
- w_in: bfloat16 [1536, 512], replicated, may hold values from -0.15625 to 0.15625
- w_mid: bfloat16 [512, 512], replicated, may hold values from -0.25 to 0.25
- w_out: bfloat16 [512, 1536], replicated, may hold values from -0.25 to 0.25
- moment_one: float32 [1835008], P(('role', 'gx', 'gy')), may hold values from -5 to 5
- moment_two: float32 [1835008], P(('role', 'gx', 'gy')), may hold values from 0.01 to 0.1
- picks: int32 [8192], P(('role', 'gx', 'gy')), may hold values from 0 to 59
- owners: int32 [8192], P(('role', 'gx', 'gy')), may hold values from 0 to 15
- counts: int32 [16, 16], P(('role', 'gy'), 'gx'), may hold values from 1 to 32, 256 in all within a row
Outputs:
- velocity_next: float32 [3, 384, 384, 128], P(None, 'gx', ('role', 'gy'))
- direction: float32 [1835008], P(('role', 'gx', 'gy'))
Inputs may be any that keep to these rules, and one draw needn't show every extreme that they name: Each row of counts sums to 256 and its largest entry is 32.
All inputs are finite; a program needn't handle non-finite values. No bound on the sum of `counts` on one device may be relied on, other than what follows from the above.
Results may differ from a plain program's by a relative error of at most 0.0085.
The roundings to bfloat16 on the way count: a program that leaves them out, or rounds other values in their place, can miss the bound.
Values sent between devices are 32-bit elements; how exact they have to be, the bound alone decides.
A program may use at most 192 MiB of HBM per device.

v0:
```python
import jax
import jax.numpy as jnp
from jax import lax
from jax.sharding import PartitionSpec as P

BLOCK = 8
ADAM_STEP = 10


TIME_STEP = 0.2
VISCOSITY = 0.05
BETA_ONE = 0.9
BETA_TWO = 0.999
EPSILON = 1e-08


def extended(x, sides, width):
    for axis, dim in sides:
        size, length = (lax.axis_size(axis), x.shape[dim])
        up = [(i, (i + 1) % size) for i in range(size)]
        down = [(j, i) for i, j in up]
        last = lax.slice_in_dim(x, length - width, length, axis=dim)
        leading = lax.slice_in_dim(x, 0, width, axis=dim)
        before = lax.ppermute(last, axis, up)
        after = lax.ppermute(leading, axis, down)
        x = jnp.concatenate([before, x, after], axis=dim)
    return x


def block_rows(field):
    comp_count, size_first, size_second, size_third = field.shape
    narrow = field.astype(jnp.bfloat16)
    pieces = narrow.reshape(
        comp_count, size_first // BLOCK, BLOCK, size_second // BLOCK, BLOCK, size_third
    )
    pieces = pieces.transpose(1, 3, 0, 2, 4, 5)
    pieces = pieces.reshape(
        size_first // BLOCK * (size_second // BLOCK), comp_count * BLOCK * BLOCK, size_third
    )
    pieces = jnp.swapaxes(pieces, 1, 2)
    return pieces.reshape(-1, comp_count * BLOCK * BLOCK * BLOCK)


def field_back(rows_out, shape):
    comp_count, size_first, size_second, size_third = shape
    pieces = rows_out.reshape(
        size_first // BLOCK * (size_second // BLOCK), size_third, comp_count * BLOCK * BLOCK
    )
    pieces = jnp.swapaxes(pieces, 1, 2)
    pieces = pieces.reshape(
        size_first // BLOCK, size_second // BLOCK, comp_count, BLOCK, BLOCK, size_third
    )
    pieces = pieces.transpose(2, 0, 3, 1, 4, 5)
    return pieces.reshape(comp_count, size_first, size_second, size_third)


def closure_rows(rows_now, w_first, w_mid, w_last):
    hidden_one = jax.nn.gelu(jnp.dot(rows_now, w_first, preferred_element_type=jnp.float32)).astype(
        jnp.bfloat16
    )
    hidden_two = jax.nn.gelu(jnp.dot(hidden_one, w_mid, preferred_element_type=jnp.float32)).astype(
        jnp.bfloat16
    )
    return jnp.dot(hidden_two, w_last, preferred_element_type=jnp.float32)


def tendency(field, rows_now, w_first, w_mid, w_last):
    padded = extended(field, (("gx", 1), (("role", "gy"), 2)), 1)
    closed = field_back(closure_rows(rows_now, w_first, w_mid, w_last), field.shape)
    first_up = padded[:, 2:, 1:-1]
    first_down = padded[:, :-2, 1:-1]
    second_up = padded[:, 1:-1, 2:]
    second_down = padded[:, 1:-1, :-2]
    third_up = jnp.roll(field, -1, 3)
    third_down = jnp.roll(field, 1, 3)
    advect = (
        field[0:1] * ((first_up - first_down) * 0.5)
        + field[1:2] * ((second_up - second_down) * 0.5)
        + field[2:3] * ((third_up - third_down) * 0.5)
    )
    spread = (
        first_up + first_down + (second_up + second_down) + (third_up + third_down) - 6.0 * field
    )
    return VISCOSITY * spread - advect + closed


def gelu_back(pre_act, upstream):
    unused_value, pull_back = jax.vjp(jax.nn.gelu, pre_act)
    return pull_back(upstream)[0]


def gradient(inputs, targets, row_weight, w_first, w_mid, w_last):
    hidden_size = w_mid.shape[0]
    pre_one = jnp.dot(inputs, w_first, preferred_element_type=jnp.float32)
    hidden_one = jax.nn.gelu(pre_one).astype(jnp.bfloat16)
    pre_two = jnp.dot(hidden_one, w_mid, preferred_element_type=jnp.float32)
    hidden_two = jax.nn.gelu(pre_two).astype(jnp.bfloat16)
    output = jnp.dot(hidden_two, w_last, preferred_element_type=jnp.float32)
    upstream = (2.0 * row_weight[:, None] * (output - targets.astype(jnp.float32))).astype(
        jnp.bfloat16
    )
    grad_out = jnp.dot(hidden_two.T, upstream, preferred_element_type=jnp.float32)
    back_two = gelu_back(
        pre_two, jnp.dot(upstream, w_last.T, preferred_element_type=jnp.float32)
    ).astype(jnp.bfloat16)
    grad_mid = jnp.dot(hidden_one.T, back_two, preferred_element_type=jnp.float32)
    back_one = gelu_back(
        pre_one, jnp.dot(back_two, w_mid.T, preferred_element_type=jnp.float32)
    ).astype(jnp.bfloat16)
    grad_in = jnp.dot(inputs.T, back_one, preferred_element_type=jnp.float32)
    grad_in = grad_in.reshape(BLOCK, 3, BLOCK, BLOCK, hidden_size).transpose(1, 2, 3, 0, 4)
    grad_out = grad_out.reshape(hidden_size, BLOCK, 3, BLOCK, BLOCK).transpose(0, 2, 3, 4, 1)
    return jnp.concatenate([grad_in.reshape(-1), grad_mid.reshape(-1), grad_out.reshape(-1)])


def adam_direction(moment_one, moment_two, grad_flat):
    moment_new = BETA_ONE * moment_one + (1.0 - BETA_ONE) * grad_flat
    second_new = BETA_TWO * moment_two + (1.0 - BETA_TWO) * grad_flat * grad_flat
    corrected = moment_new / (1.0 - BETA_ONE**ADAM_STEP)
    return corrected / (jnp.sqrt(second_new / (1.0 - BETA_TWO**ADAM_STEP)) + EPSILON)


def local(
    velocity, target_field, w_in, w_mid, w_out, moment_one, moment_two, picks, owners, counts
):
    groups = lax.axis_size("gx")
    hidden_size = w_mid.shape[0]
    close_width = w_in.shape[0]
    w_first = (
        w_in.reshape(3, BLOCK, BLOCK, BLOCK, hidden_size)
        .transpose(3, 0, 1, 2, 4)
        .reshape(close_width, hidden_size)
    )
    w_last = (
        w_out.reshape(hidden_size, 3, BLOCK, BLOCK, BLOCK)
        .transpose(0, 4, 1, 2, 3)
        .reshape(hidden_size, close_width)
    )
    comp_count, size_first, size_second, size_third = velocity.shape
    first_rows = block_rows(velocity)
    section_one = velocity + TIME_STEP * tendency(velocity, first_rows, w_first, w_mid, w_last)
    second_rows = block_rows(section_one)
    velocity_next = 0.75 * velocity + 0.25 * (
        section_one + TIME_STEP * tendency(section_one, second_rows, w_first, w_mid, w_last)
    )
    blocks_second = size_second // BLOCK
    blocks_third = size_third // BLOCK
    mid_span = blocks_second - 1
    last_span = blocks_third - 1
    anchor_first = picks // (mid_span * last_span)
    anchor_second = picks // last_span % mid_span
    anchor_third = picks % last_span
    corner = jnp.arange(8, dtype=jnp.int32)
    block_index = (
        (anchor_first[:, None] + corner // 4) * blocks_second
        + anchor_second[:, None]
        + corner // 2 % 2
    ) * blocks_third
    block_index = block_index + anchor_third[:, None] + corner % 2
    pick_count = counts[0, 0]
    slot_count = picks.shape[0]
    alive_mask = jnp.arange(slot_count, dtype=jnp.int32) < pick_count
    trainer_ids = jnp.arange(groups, dtype=jnp.int32)
    match = (owners[:, None] == trainer_ids[None, :]) & alive_mask[:, None]
    totals = lax.psum(jnp.sum(match.astype(jnp.float32), axis=0), "gx")
    inverse = 1.0 / jnp.maximum(totals, 1.0)
    target_rows = block_rows(target_field)
    flat_index = block_index.reshape(-1)
    rows_in = first_rows[flat_index]
    rows_target = target_rows[flat_index]
    patch_weight = jnp.sum(jnp.where(match, inverse[None, :], 0.0), axis=1)
    row_weight = jnp.repeat(patch_weight, 8)
    grad_flat = gradient(rows_in, rows_target, row_weight, w_first, w_mid, w_last)
    shard_len = moment_one.shape[0]
    grad_whole = lax.psum(grad_flat, ("role", "gx", "gy"))
    local_grad = lax.dynamic_slice_in_dim(
        grad_whole, lax.axis_index(("role", "gx", "gy")) * shard_len, shard_len
    )
    direction = adam_direction(moment_one, moment_two, local_grad)
    return (velocity_next, direction)


def solution(mesh):
    return jax.shard_map(
        local,
        mesh=mesh,
        in_specs=(
            P(None, "gx", ("role", "gy"), None),
            P(None, "gx", ("role", "gy"), None),
            P(),
            P(),
            P(),
            P(("role", "gx", "gy")),
            P(("role", "gx", "gy")),
            P(("role", "gx", "gy")),
            P(("role", "gx", "gy")),
            P(("role", "gy"), "gx"),
        ),
        out_specs=(P(None, "gx", ("role", "gy"), None), P(("role", "gx", "gy"))),
        check_vma=False,
    )
```

profile of v0, /device:TPU:4, one launch (start us, length us, event | category | flops | bytes accessed | tf_op | source)
XLA Modules:
  0.0 464.7 jit_solution(12236564399345014882)
XLA Ops:
  7.2 1.5 fusion.128
  8.7 3.2 collective-permute-start.1
  11.9 5.4 %collective-permute-start = (f32[3,1,24,128]{3,2,1,0:T(8,128)}, f32[3,1,24,128]{3,2,1,0:T(8,128)S(1)}, u32[]{:S(2)}, u32[]{:S(2)}) collective-permute-start(f32[3,1,24,128]{3,2,1,0:T(8,128)} %get-tuple-element.17), channel_id=1, source_target_pairs={{8,0},{16,8},{24,16},{32,24},{40,32},{48,40},{56,48},{64,56},{72,6... | collective-permute-start | bytes 110600 | tf_op jit(solution)/shard_map/ppermute | solution.py:25
  17.3 3.0 fusion.129
  20.3 1.5 fusion.130
  22.9 40.3 %psum.14 = f32[16]{0:T(128)S(1)} all-reduce(f32[16]{0:T(128)S(1)} %convert_reduce_fusion), channel_id=1, replica_groups=mesh['role'=2,'gx'=16,'gy'=8] {'gx'}, use_global_device_ids=true, to_apply=%region_1.2 | all-reduce | flops 16 | bytes 128 | tf_op jit(solution)/shard_map/psum | solution.py:165
  63.2 1.7 copy.61
  65.0 1.6 copy.62
  68.0 1.1 copy.71
  69.1 1.6 reshape.252
  70.9 2.1 gather_fusion.1
  74.1 1.1 copy.59
  75.2 1.6 reshape.236
  76.8 2.2 gather_fusion
  78.9 1.8 fusion.135
  81.1 1.2 copy-done.3
  83.0 2.4 fusion.122
  85.3 0.8 fusion.15
  86.8 1.4 convolution_bitcast_fusion
  88.2 4.1 fusion.51
  92.3 38.4 %copy.74 = f32[512,3,8,8,8]{4,3,2,1,0:T(8,128)} copy(f32[512,3,8,8,8]{0,3,2,1,4:T(8,128)} %bitcast.85) | data formatting | bytes 6291456 | tf_op jit(solution)/shard_map/transpose | solution.py:112
  130.8 34.9 %reshape.257 = f32[786432]{0:T(1024)} reshape(f32[512,3,8,8,8]{4,3,2,1,0:T(8,128)} %copy.74) | data formatting | bytes 6291456 | tf_op jit(solution)/shard_map/reshape | solution.py:113
  165.6 1.5 copy.77
  167.1 4.6 copy.72
  171.7 0.8 copy.76
  172.6 1.0 copy-done.4
  173.6 8.7 %pad_maximum_fusion = f32[1835008]{0:T(1024)} fusion(f32[786432]{0:T(1024)S(1)} %copy-done.4, f32[262144]{0:T(1024)S(1)} %bitcast.96, f32[786432]{0:T(1024)S(1)} %bitcast.90), kind=kLoop, calls=%fused_computation.2 | loop fusion | flops 3670016 | bytes 14680064 | tf_op jit(solution)/shard_map/concatenate | solution.py:113
  182.3 1.0 multiply_bitcast_fusion.2
  183.9 1.8 fusion.124
  186.3 2.3 collective-permute-start.2
  188.6 1.1 fusion.133
  189.7 2.5 fusion.67
  192.6 1.3 copy.63
  193.9 1.4 copy.64
  195.6 3.2 fusion.123
  200.0 3.3 collective-permute-start.5
  203.2 1.8 fusion.134
  205.1 1.5 fusion.126
  206.6 3.1 fusion.59
  209.7 1.5 fusion.127
  211.9 2.0 collective-permute-start.7
  214.0 1.0 fusion.50
  214.9 1.5 reshape.247
  216.5 1.3 copy.67
  217.8 1.4 copy.68
  219.5 3.8 multiply_add_fusion
  223.3 233.2 %all-reduce.2.cloned.1.call-done = f32[1835008]{0:T(1024)} async-done(((f32[1835008]{0:T(1024)}), f32[1835008]{0:T(1024)}) %all-reduce.2.cloned.1.call-update) | async-done | bytes 7340048 | tf_op jit(solution)/shard_map/psum | solution.py:175
  456.5 1.4 fusion.95
  (81 shorter events, 9.0 us)
Async XLA Ops:
  7.2 73.5 %copy-start = (bf16[512,512]{1,0:T(8,128)(2,1)S(1)}, bf16[512,512]{1,0:T(8,128)(2,1)}, u32[]{:S(2)}) copy-start(bf16[512,512]{1,0:T(8,128)(2,1)} %param.13) | copy-start | bytes 1572868
  7.2 449.3 %all-reduce.2.cloned.1.call-start = ((), (), s32[]{:S(2)}) async-start(), calls=%async_computation | async-start | bytes 14680064 | tf_op jit(solution)/shard_map/psum | solution.py:175
  8.7 64.3 %collective-permute-start.1 = (f32[3,1,24,128]{3,2,1,0:T(8,128)}, f32[3,1,24,128]{3,2,1,0:T(8,128)S(1)}, u32[]{:S(2)}, u32[]{:S(2)}) collective-permute-start(f32[3,1,24,128]{3,2,1,0:T(8,128)} %get-tuple-element.18), channel_id=1, source_target_pairs={{0,8},{8,16},{16,24},{24,32},{32,40},{40,48},{48,56},{56,64},{64,7... | collective-permute-start | bytes 110600 | tf_op jit(solution)/shard_map/ppermute | solution.py:24
  11.9 8.4 %copy-start.1 = (f32[3,24,24,128]{3,2,1,0:T(8,128)S(1)}, f32[3,24,24,128]{3,2,1,0:T(8,128)}, u32[]{:S(2)}) copy-start(f32[3,24,24,128]{3,2,1,0:T(8,128)} %param.10) | copy-start | bytes 2654212
  11.9 171.4 %collective-permute-start = (f32[3,1,24,128]{3,2,1,0:T(8,128)}, f32[3,1,24,128]{3,2,1,0:T(8,128)S(1)}, u32[]{:S(2)}, u32[]{:S(2)}) collective-permute-start(f32[3,1,24,128]{3,2,1,0:T(8,128)} %get-tuple-element.17), channel_id=1, source_target_pairs={{8,0},{16,8},{24,16},{32,24},{40,32},{48,40},{56,48},{64,56},{72,6... | collective-permute-start | bytes 110600 | tf_op jit(solution)/shard_map/ppermute | solution.py:25
  20.3 1.5 copy-start.18
  20.3 2.5 copy-start.19
  65.0 1.7 copy-start.11
  66.6 1.2 copy-start.14
  67.8 120.8 %copy-start.2 = (bf16[8,3,8,8,512]{4,3,2,1,0:T(8,128)(2,1)}, bf16[8,3,8,8,512]{4,3,2,1,0:T(8,128)(2,1)S(1)}, u32[]{:S(2)}) copy-start(bf16[8,3,8,8,512]{4,3,2,1,0:T(8,128)(2,1)S(1)} %copy.60) | copy-start | bytes 4718596
  73.2 0.9 copy-start.12
  78.9 2.2 copy-start.15
  80.7 5.4 %copy-start.5 = (f32[256,512]{1,0:T(8,128)}, f32[256,512]{1,0:T(8,128)S(1)}, u32[]{:S(2)}) copy-start(f32[256,512]{1,0:T(8,128)S(1)} %fusion.135) | copy-start | bytes 1572868
  80.7 1.6 copy-start.3
  86.1 0.7 copy-start.13
  171.7 1.9 copy-start.4
  185.6 9.6 %collective-permute-start.3 = (f32[3,26,1,128]{3,2,1,0:T(1,128)}, f32[3,26,1,128]{3,2,1,0:T(1,128)}, u32[]{:S(2)}, u32[]{:S(2)}) collective-permute-start(f32[3,26,1,128]{3,2,1,0:T(1,128)} %get-tuple-element.7), channel_id=1, source_target_pairs={{0,1},{1,2},{2,3},{3,4},{4,5},{5,6},{6,7},{7,128},{128,129},{129,1... | collective-permute-start | bytes 119816 | tf_op jit(solution)/shard_map/ppermute | solution.py:24
  186.3 8.9 %collective-permute-start.2 = (f32[3,26,1,128]{3,2,1,0:T(1,128)}, f32[3,26,1,128]{3,2,1,0:T(1,128)}, u32[]{:S(2)}, u32[]{:S(2)}) collective-permute-start(f32[3,26,1,128]{3,2,1,0:T(1,128)} %get-tuple-element.6), channel_id=1, source_target_pairs={{1,0},{2,1},{3,2},{4,3},{5,4},{6,5},{7,6},{128,7},{129,128},{130,1... | collective-permute-start | bytes 119816 | tf_op jit(solution)/shard_map/ppermute | solution.py:25
  192.6 2.7 copy-start.6
  193.9 1.4 copy-start.7
  193.9 1.7 copy-start.8
  199.6 11.6 %collective-permute-start.4 = (f32[3,1,24,128]{3,2,1,0:T(8,128)S(1)}, f32[3,1,24,128]{3,2,1,0:T(8,128)S(1)}, u32[]{:S(2)}, u32[]{:S(2)}) collective-permute-start(f32[3,1,24,128]{3,2,1,0:T(8,128)S(1)} %get-tuple-element.12), channel_id=1, source_target_pairs={{8,0},{16,8},{24,16},{32,24},{40,32},{48,40},{56,48},{64,56},{72,6... | collective-permute-start | bytes 110600 | tf_op jit(solution)/shard_map/ppermute | solution.py:25
  200.0 11.3 %collective-permute-start.5 = (f32[3,1,24,128]{3,2,1,0:T(8,128)S(1)}, f32[3,1,24,128]{3,2,1,0:T(8,128)S(1)}, u32[]{:S(2)}, u32[]{:S(2)}) collective-permute-start(f32[3,1,24,128]{3,2,1,0:T(8,128)S(1)} %get-tuple-element.11), channel_id=1, source_target_pairs={{0,8},{8,16},{16,24},{24,32},{32,40},{40,48},{48,56},{56,64},{64,7... | collective-permute-start | bytes 110600 | tf_op jit(solution)/shard_map/ppermute | solution.py:24
  211.9 7.2 %collective-permute-start.6 = (f32[3,26,1,128]{3,2,1,0:T(1,128)}, f32[3,26,1,128]{3,2,1,0:T(1,128)}, u32[]{:S(2)}, u32[]{:S(2)}) collective-permute-start(f32[3,26,1,128]{3,2,1,0:T(1,128)} %get-tuple-element.5), channel_id=1, source_target_pairs={{1,0},{2,1},{3,2},{4,3},{5,4},{6,5},{7,6},{128,7},{129,128},{130,1... | collective-permute-start | bytes 119816 | tf_op jit(solution)/shard_map/ppermute | solution.py:25
  211.9 7.2 %collective-permute-start.7 = (f32[3,26,1,128]{3,2,1,0:T(1,128)}, f32[3,26,1,128]{3,2,1,0:T(1,128)}, u32[]{:S(2)}, u32[]{:S(2)}) collective-permute-start(f32[3,26,1,128]{3,2,1,0:T(1,128)} %get-tuple-element.4), channel_id=1, source_target_pairs={{0,1},{1,2},{2,3},{3,4},{4,5},{5,6},{6,7},{7,128},{128,129},{129,1... | collective-permute-start | bytes 119816 | tf_op jit(solution)/shard_map/ppermute | solution.py:24
  217.7 1.5 copy-start.9
  217.7 1.8 copy-start.10
  219.5 237.0 %copy-start.16 = (f32[7168]{0:T(1024)S(1)}, f32[7168]{0:T(1024)}, u32[]{:S(2)}) copy-start(f32[7168]{0:T(1024)} %param.16) | copy-start | bytes 86020
  219.5 237.0 %copy-start.17 = (f32[7168]{0:T(1024)S(1)}, f32[7168]{0:T(1024)}, u32[]{:S(2)}) copy-start(f32[7168]{0:T(1024)} %param.15) | copy-start | bytes 86020
Sparse Core Ops, SparseCore 0:
  182.5 273.9 all-reduce.1
where the time goes:
time: 466 us; the launch traced here: 465 us
  waiting for transfers between devices  233 us (50%)
  local copies, waits for them, and re-layouts  119 us (26%)
  blocking collectives  40.3 us (9%)
  other arithmetic  20.1 us (4%)
  matrix products  20 us (4%)
  starting transfers between devices  17.1 us (4%)
  between operations  15 us (3%)
    psum x1, waiting for transfers between devices, local(): grad_whole = lax.psum(grad_flat, ('role', 'gx', 'gy'))  233 us
    psum x1, blocking collectives, local(): totals = lax.psum(jnp.sum(match.astype(jnp.float32), axis=0), 'gx')  40.3 us
    transpose x1, local copies, waits for them, and re-layouts, gradient(): grad_out.reshape(hidden_size, BLOCK, 3, BLOCK, BLOCK)  38.4 us
    reshape x1, local copies, waits for them, and re-layouts, gradient(): grad_out.reshape(-1)  34.9 us
  transfers between devices with their start and end apart: 9, of which 1 were waited for; matrix products, arithmetic and copies ran while one was open for 33% of the time, Pallas kernels for 0%

commit v1 on v0

v1 whole, which is shorter than its diff:
```python
import math

import jax
import jax.numpy as jnp
from jax import lax
from jax.experimental import pallas as pl
from jax.experimental.pallas import tpu as pltpu
from jax.sharding import PartitionSpec as P

ADAM_STEP = 10
TIME_STEP = 0.2
VISCOSITY = 0.05
BETA_ONE = 0.9
BETA_TWO = 0.999
EPSILON = 1e-08
MESH = pl.DeviceIdType.MESH
F32 = jnp.float32
BF16 = jnp.bfloat16
NN = (((1,), (0,)), ((), ()))
NT = (((1,), (1,)), ((), ()))
TN = (((0,), (0,)), ((), ()))
GELU_K = math.sqrt(2.0 / math.pi)
GELU_C = 0.044715
ROWS = 144
WIDE = 1536


def dot(a, b, dims=NN):
    return lax.dot_general(a, b, dims, preferred_element_type=F32)


def gelu(a):
    t = jnp.tanh(GELU_K * (a + GELU_C * (a * a * a)))
    return a * (0.5 * (1.0 + t))


def gelu_and_slope(a):
    a2 = a * a
    t = jnp.tanh(GELU_K * (a + GELU_C * (a2 * a)))
    cdf = 0.5 * (1.0 + t)
    slope = cdf + (0.5 * GELU_K) * a * (1.0 - t * t) * (1.0 + (3.0 * GELU_C) * a2)
    return a * cdf, slope


def place(r, z, yh, x, yl):
    return {"role": r, "gx": z * 2 + yh, "gy": x * 2 + yl}


def kernel(
    vel_hbm, tgt_hbm, win_hbm, wmid_hbm, wout_hbm, mom1, mom2, picks, owners, counts,
    next_hbm, direction,
    vp, sp, vnext, tgt, w_in, w_mid, w_out, w_first, w_last, perm,
    t_zero, t_one, xf, xb, yf, info, weight, hist_out, hist, ysend, yrecv,
    xs, ys, slope_one, slope_two, h_one, h_two, e_all, b_two, b_one,
    grad, rx, ry, rz, sx, sy, sz, rx2, ry2, rz2, sxy, sz2, rxy3, rz3,
    load_sem, send_sem, recv_sem,
):
    r = lax.axis_index("role")
    i = lax.axis_index("gx")
    j = lax.axis_index("gy")
    z, yh, x, yl = i // 2, i % 2, j // 2, j % 2
    y = yh * 2 + yl
    q = r * 8 + j

    def at_q(k):
        k = lax.rem(k + 16, 16)
        return {"role": k // 8, "gx": i, "gy": k % 8}

    def at_i(k):
        return {"role": r, "gx": lax.rem(k + 16, 16), "gy": j}

    def along_x(d):
        return place(r, z, yh, lax.rem(x + d, 4), yl)

    def along_y(d):
        k = lax.rem(y + d, 4)
        return place(r, z, k // 2, x, k % 2)

    def along_z(d):
        return place(r, lax.rem(z + d, 8), yh, x, yl)

    pair = {"role": 1 - r, "gx": i, "gy": j}

    loads = []

    def load(src, dst):
        c = pltpu.make_async_copy(src, dst, load_sem.at[len(loads)])
        c.start()
        loads.append(c)
        return c

    load_v = load(vel_hbm, vp.at[:, 1:25, 8:32, :])
    load_t = load(tgt_hbm, tgt)
    load_wi = load(win_hbm, w_in)
    load_wo = load(wout_hbm, w_out)
    load_wm = load(wmid_hbm, w_mid)

    barrier = pltpu.get_barrier_semaphore()
    other = at_q(q + 2 * yl - 1)
    for d in range(1, 16):
        pl.semaphore_signal(barrier, inc=1, device_id=at_i(i + d), device_id_type=MESH)
    for d in range(1, 4):
        pl.semaphore_signal(barrier, inc=1, device_id=along_x(d), device_id_type=MESH)
    for who in (place(r, z, yh, x, 1 - yl), place(r, z, 1 - yh, x, 1 - yl), pair, other):
        pl.semaphore_signal(barrier, inc=1, device_id=who, device_id_type=MESH)

    def column(row):
        a = lax.broadcasted_iota(jnp.int32, (32, 32), 0)
        b = lax.broadcasted_iota(jnp.int32, (32, 32), 1)
        picked = jnp.where(a == b, jnp.broadcast_to(row, (32, 32)), 0.0)
        return jnp.broadcast_to(jnp.sum(picked, axis=1, keepdims=True), (32, 128))

    o = picks[...]
    one, nil = jnp.ones_like(o), jnp.zeros_like(o)
    over30 = jnp.where(o >= 30, one, nil)
    over15 = jnp.where(o >= 15, one, nil) + over30 + jnp.where(o >= 45, one, nil)
    first_block = (over30 * 3 + (over15 - 2 * over30)) * 16 + (o - 15 * over15)
    info[0] = column(first_block.astype(F32))
    owner = column(owners[...].astype(F32))
    slot = lax.broadcasted_iota(jnp.int32, (32, 128), 0)
    lane = lax.broadcasted_iota(jnp.int32, (32, 128), 1).astype(F32)
    alive = slot < jnp.broadcast_to(counts[...], (32, 128))
    match = jnp.where(alive, jnp.where(lane == owner, 1.0, 0.0), 0.0)
    hist_out[...] = jnp.broadcast_to(jnp.sum(match, axis=0, keepdims=True), (8, 128))
    hist[pl.ds(i, 1)] = hist_out[...].reshape(1, 8, 128)

    count = [0]

    def send(src, dst, who):
        k = count[0]
        count[0] += 1
        c = pltpu.make_async_remote_copy(
            src_ref=src, dst_ref=dst, send_sem=send_sem.at[k], recv_sem=recv_sem.at[k],
            device_id=who, device_id_type=MESH,
        )
        c.start()
        return c

    pl.semaphore_wait(barrier, 22)

    hist_copies = [send(hist_out, hist.at[i], at_i(i + d)) for d in range(1, 16)]
    pair_info = send(info.at[0], info.at[1], pair)

    def halo_start(field, slot):
        flat = field.reshape(3 * 26 * 40, 128)
        for c in range(3):
            ysend[slot, 0, c] = flat[pl.ds((c * 26 + 1) * 40 + 8, 24, stride=40), :]
            ysend[slot, 1, c] = flat[pl.ds((c * 26 + 1) * 40 + 31, 24, stride=40), :]
        return [
            send(field.at[:, 1, 8:32, :], field.at[:, 25, 8:32, :], at_i(i - 1)),
            send(field.at[:, 24, 8:32, :], field.at[:, 0, 8:32, :], at_i(i + 1)),
            send(ysend.at[slot, 0], yrecv.at[slot, 1], at_q(q - 1)),
            send(ysend.at[slot, 1], yrecv.at[slot, 0], at_q(q + 1)),
        ]

    def halo_finish(field, slot, copies):
        for c in copies:
            c.wait_recv()
        flat = field.reshape(3 * 26 * 40, 128)
        for c in range(3):
            flat[pl.ds((c * 26 + 1) * 40 + 7, 24, stride=40), :] = yrecv[slot, 0, c]
            flat[pl.ds((c * 26 + 1) * 40 + 32, 24, stride=40), :] = yrecv[slot, 1, c]

    def turn(take):
        def body(k, carry):
            d = take(k // 3, k % 3).reshape(192, 128)
            rows = pl.ds(pl.multiple_of(k * 128, 128), 128)
            t_zero[rows, :] = d[:128].T
            t_one[rows, 0:64] = d[128:].T
            return carry

        lax.fori_loop(0, 9, body, 0)

    def take_from(field):
        def take(bx, by):
            return field[:, pl.ds(bx * 8 + 1, 8), pl.ds(pl.multiple_of(by * 8 + 8, 8), 8), :]

        return take

    half = lax.broadcasted_iota(jnp.int32, (ROWS, 128), 1)

    def rows_of(write):
        for oz in range(8):
            write(oz * 128, t_zero[pl.ds(oz, ROWS, stride=8), :])
        for k in range(4):
            a = t_one[pl.ds(2 * k, ROWS, stride=8), :]
            b = t_one[pl.ds(2 * k + 1, ROWS, stride=8), :]
            write(1024 + k * 128, jnp.where(half < 64, a, pltpu.roll(b, 64, 1)))

    pr = lax.broadcasted_iota(jnp.int32, (256, 256), 0)
    pc = lax.broadcasted_iota(jnp.int32, (256, 256), 1)
    perm[...] = jnp.where(pc == (pr & 31) * 8 + (pr >> 5), 1.0, 0.0).astype(BF16)

    load_t.wait()

    def take_target(bx, by):
        return tgt[:, pl.ds(bx * 8, 8), pl.ds(pl.multiple_of(by * 8, 8), 8), :]

    turn(take_target)
    for g in range(6):
        tiles = []
        src, base = (t_zero, g) if g < 4 else (t_one, g - 4)
        for quad in range(2):
            tile = None
            for m in range(4):
                part = src[pl.ds(4 * quad + m, ROWS, stride=8), :]
                shift = (32 * (m - base)) % 128
                if shift:
                    part = pltpu.roll(part, shift, 1)
                tile = part if tile is None else jnp.where(half >= 32 * m, part, tile)
            tiles.append(tile.astype(BF16))
        yf[0, :, 256 * g : 256 * g + 256] = dot(jnp.concatenate(tiles, axis=1), perm[...])
    pair_y = send(yf.at[0], yf.at[1], pair)

    load_v.wait()
    halo_one = halo_start(vp, 0)
    turn(take_from(vp))

    def write_x(at, tile):
        xf[0, :, at : at + 128] = tile
        xb[0, :, at : at + 128] = tile.astype(BF16)

    rows_of(write_x)
    pair_x = send(xf.at[0], xf.at[1], pair)

    for c in hist_copies:
        c.wait_recv()
    totals = jnp.sum(hist[...], axis=0)
    inverse = 1.0 / jnp.maximum(totals, 1.0)
    own_weight = jnp.sum(match * inverse[0:1, :], axis=1, keepdims=True)
    weight[0] = jnp.broadcast_to(own_weight, (32, 128))
    pair_w = send(weight.at[0], weight.at[1], pair)

    load_wi.wait()
    load_wo.wait()
    load_wm.wait()
    for g in range(6):
        wi = dot(perm[...], w_in[256 * g : 256 * g + 256, :]).astype(BF16)
        wo = dot(perm[...], w_out[:, 256 * g : 256 * g + 256], NT).astype(BF16)
        for oz in range(8):
            at = oz * 128 + 32 * g if g < 4 else 1024 + oz * 64 + 32 * (g - 4)
            w_first[at : at + 32, :] = wi[32 * oz : 32 * oz + 32]
            w_last[at : at + 32, :] = wo[32 * oz : 32 * oz + 32]

    for c in (pair_info, pair_y, pair_x, pair_w):
        c.wait_recv()

    def side(s, carry):
        rows = pl.ds(pl.multiple_of(s * 256, 256), 256)

        @pl.when(s == 1)
        def _():
            xb[1] = xf[1].astype(BF16)

        start = info[s]
        start = jnp.concatenate([start, start], axis=1)[:, :ROWS]
        block = lax.broadcasted_iota(jnp.int32, (32, ROWS), 1).astype(F32)
        chosen = jnp.concatenate(
            [
                jnp.where(block == start + float(k // 4 * 48 + k // 2 % 2 * 16 + k % 2), 1.0, 0.0)
                for k in range(8)
            ],
            axis=0,
        ).astype(BF16)
        for n in range(3):
            cols = slice(512 * n, 512 * n + 512)
            xs[rows, cols] = dot(chosen, xb[s, :, cols]).astype(BF16)
        a, slope = gelu_and_slope(dot(xs[rows, :], w_first[...]))
        slope_one[rows, :] = slope
        h1 = a.astype(BF16)
        h_one[rows, :] = h1
        a, slope = gelu_and_slope(dot(h1, w_mid[...]))
        h2 = a.astype(BF16)
        h_two[rows, :] = h2
        w8 = 2.0 * jnp.concatenate([weight[s]] * 8, axis=0)
        w8 = jnp.concatenate([w8] * 4, axis=1)
        up = None
        for n in range(3):
            cols = slice(512 * n, 512 * n + 512)
            target = dot(chosen, yf[s, :, cols].astype(BF16))
            e = (w8 * (dot(h2, w_out[:, cols]) - target)).astype(BF16)
            e_all[rows, cols] = e
            part = dot(e, w_out[:, cols], NT)
            up = part if up is None else up + part
        b_two[rows, :] = (slope * up).astype(BF16)
        return carry

    lax.fori_loop(0, 2, side, 0)

    def put(value, start, stride, size):
        for cb in range(value.shape[1] // 128):
            grad_flat[pl.ds(start + cb, size, stride=stride), :] = value[:, cb * 128 : cb * 128 + 128]

    grad_flat = grad.reshape(7168, 128)

    @pl.when(r == 0)
    def _():
        for s in range(2):
            rows = slice(256 * s, 256 * s + 256)
            up = dot(b_two[rows, :], w_mid[...], NT)
            b_one[rows, :] = (slope_one[rows, :] * up).astype(BF16)
        for k in range(4):
            part = dot(xs[:, 256 * k : 256 * k + 256], b_one[...], TN)
            put(part[:128], 8 * k, 32, 128)
            put(part[128:], 8 * k + 4, 32, 128)
        for k in range(2):
            part = dot(xs[:, 1024 + 256 * k : 1280 + 256 * k], b_one[...], TN)
            for m in range(4):
                put(part[64 * m : 64 * m + 64], 4096 + 4 * (4 * k + m), 32, 64)
        put(dot(h_one[:, 0:256], b_two[...], TN), 6144, 4, 256)

    @pl.when(r == 1)
    def _():
        for k in range(2):
            for n in range(3):
                part = dot(h_two[:, 256 * k : 256 * k + 256], e_all[:, 512 * n : 512 * n + 512], TN)
                put(part, 1024 + 3072 * k + 4 * n, 12, 256)
        put(dot(h_one[:, 256:512], b_two[...], TN), 0, 4, 256)

    gx5 = grad.reshape(16, 4, 2, 56, 128)
    gy6 = grad.reshape(8, 2, 4, 2, 56, 128)
    gz = grad.reshape(8, 16, 56, 128)
    copies_x, copies_y, copies_z = [], [], []
    for d in range(1, 4):
        copies_x.append(send(gx5.at[:, lax.rem(x + d, 4), :, 0:24, :], rx.at[d - 1], along_x(d)))
        k = lax.rem(y + d, 4)
        copies_y.append(send(gy6.at[:, k // 2, :, k % 2, 24:48, :], ry.at[d - 1], along_y(d)))
    for d in range(1, 8):
        copies_z.append(send(gz.at[lax.rem(z + d, 8), :, 48:56, :], rz.at[d - 1], along_z(d)))

    def closure(rows):
        q1 = gelu(dot(rows, w_first[...])).astype(BF16)
        q2 = gelu(dot(q1, w_mid[...])).astype(BF16)
        for n in range(2):
            out = dot(q2, w_last[512 * n : 512 * n + 512, :], NT)
            for m in range(4):
                t_zero[pl.ds(4 * n + m, ROWS, stride=8), :] = out[:, 128 * m : 128 * m + 128]
        out = dot(q2, w_last[1024:1536, :], NT)
        for m in range(4):
            tile = out[:, 128 * m : 128 * m + 128]
            t_one[pl.ds(2 * m, ROWS, stride=8), :] = tile
            t_one[pl.ds(2 * m + 1, ROWS, stride=8), :] = pltpu.roll(tile, 64, 1)

    def section(field, finish):
        def body(k, carry):
            bx, by = k // 3, k % 3
            rows = pl.ds(pl.multiple_of(k * 128, 128), 128)
            closed = [None, None, None]
            front = t_zero[rows, :].T
            closed[0] = front[:64].reshape(8, 8, 128)
            closed[1] = front[64:].reshape(8, 8, 128)
            closed[2] = t_one[rows, :].T[:64].reshape(8, 8, 128)
            here = pl.ds(pl.multiple_of(by * 8 + 8, 8), 8)
            around = pl.ds(pl.multiple_of(by * 8, 8), 24)
            center = [field[c, pl.ds(bx * 8 + 1, 8), here, :] for c in range(3)]
            for c in range(3):
                mid = center[c]
                first_up = field[c, pl.ds(bx * 8 + 2, 8), here, :]
                first_down = field[c, pl.ds(bx * 8, 8), here, :]
                window = field[c, pl.ds(bx * 8 + 1, 8), around, :]
                second_up = window[:, 9:17, :]
                second_down = window[:, 7:15, :]
                third_up = pltpu.roll(mid, 127, 2)
                third_down = pltpu.roll(mid, 1, 2)
                advect = (
                    center[0] * ((first_up - first_down) * 0.5)
                    + center[1] * ((second_up - second_down) * 0.5)
                    + center[2] * ((third_up - third_down) * 0.5)
                )
                spread = (
                    first_up + first_down + (second_up + second_down) + (third_up + third_down) - 6.0 * mid
                )
                finish(c, bx, by, mid, VISCOSITY * spread - advect + closed[c])
            return carry

        lax.fori_loop(0, 9, body, 0)

    halo_finish(vp, 0, halo_one)
    closure(xb[0])

    def finish_one(c, bx, by, mid, rate):
        here = pl.ds(pl.multiple_of(by * 8 + 8, 8), 8)
        sp[c, pl.ds(bx * 8 + 1, 8), here, :] = mid + TIME_STEP * rate

    section(vp, finish_one)
    halo_two = halo_start(sp, 1)
    turn(take_from(sp))

    def write_second(at, tile):
        xb[1, :, at : at + 128] = tile.astype(BF16)

    rows_of(write_second)
    closure(xb[1])
    halo_finish(sp, 1, halo_two)

    def finish_two(c, bx, by, mid, rate):
        here = pl.ds(pl.multiple_of(by * 8 + 8, 8), 8)
        start = vp[c, pl.ds(bx * 8 + 1, 8), here, :]
        vnext[c, pl.ds(bx * 8, 8), pl.ds(pl.multiple_of(by * 8, 8), 8), :] = 0.75 * start + 0.25 * (
            mid + TIME_STEP * rate
        )

    section(sp, finish_two)
    store = pltpu.make_async_copy(vnext, next_hbm, load_sem.at[5])
    store.start()

    for c in copies_x:
        c.wait_recv()
    for k in range(16):
        sx[k] = gx5[k, x, :, 0:24, :] + (rx[0, k] + rx[1, k] + rx[2, k])
    sx6 = sx.reshape(8, 2, 2, 24, 128)
    next_x, next_y, next_z = [], [], []
    for d in range(1, 4):
        k = lax.rem(y + d, 4)
        next_x.append(send(sx6.at[:, k // 2, k % 2], rx2.at[d - 1], along_y(d)))
    for c in copies_y:
        c.wait_recv()
    for k in range(8):
        sy[k] = gy6[k, yh, :, yl, 24:48, :] + (ry[0, k] + ry[1, k] + ry[2, k])
    for d in range(1, 4):
        next_y.append(send(sy.at[:, lax.rem(x + d, 4)], ry2.at[d - 1], along_x(d)))
    for c in copies_z:
        c.wait_recv()
    total = gz[z, :, 48:56, :]
    for d in range(7):
        total = total + rz[d]
    sz[...] = total.reshape(2, 4, 2, 8, 128)
    for d in range(1, 4):
        next_z.append(send(sz.at[:, lax.rem(x + d, 4)], rz2.at[d - 1], along_x(d)))

    for c in next_x:
        c.wait_recv()
    for k in range(8):
        sxy[k, 0:24, :] = sx6[k, yh, yl] + (rx2[0, k] + rx2[1, k] + rx2[2, k])
    for c in next_y:
        c.wait_recv()
    for k in range(8):
        sxy[k, 24:48, :] = sy[k, x] + (ry2[0, k] + ry2[1, k] + ry2[2, k])
    last = [send(sxy.at[lax.rem(z + d, 8)], rxy3.at[d - 1], along_z(d)) for d in range(1, 8)]
    for c in next_z:
        c.wait_recv()
    sz2[...] = sz[:, x] + (rz2[0] + rz2[1] + rz2[2])
    last_z = []
    for d in range(1, 4):
        k = lax.rem(y + d, 4)
        last_z.append(send(sz2.at[k // 2, k % 2], rz3.at[d - 1], along_y(d)))
    for c in last + last_z:
        c.wait_recv()
    front = sxy[z]
    for d in range(7):
        front = front + rxy3[d]
    back = sz2[yh, yl] + (rz3[0] + rz3[1] + rz3[2])
    g = jnp.concatenate([front, back], axis=0)
    moment = BETA_ONE * mom1[...] + (1.0 - BETA_ONE) * g
    second = BETA_TWO * mom2[...] + (1.0 - BETA_TWO) * g * g
    corrected = moment / (1.0 - BETA_ONE**ADAM_STEP)
    direction[...] = corrected / (jnp.sqrt(second / (1.0 - BETA_TWO**ADAM_STEP)) + EPSILON)

    for c in (
        hist_copies + [pair_info, pair_y, pair_x, pair_w] + halo_one + halo_two
        + copies_x + copies_y + copies_z + next_x + next_y + next_z + last + last_z
    ):
        c.wait_send()
    store.wait()


def local(velocity, target_field, w_in, w_mid, w_out, moment_one, moment_two, picks, owners, counts):
    any_space = pl.BlockSpec(memory_space=pl.ANY)
    vmem = pl.BlockSpec(memory_space=pltpu.VMEM)
    V = pltpu.VMEM
    next_velocity, direction = pl.pallas_call(
        kernel,
        out_shape=(
            jax.ShapeDtypeStruct(velocity.shape, F32),
            jax.ShapeDtypeStruct((56, 128), F32),
        ),
        in_specs=[any_space] * 5 + [vmem] * 5,
        out_specs=(any_space, vmem),
        scratch_shapes=[
            V((3, 26, 40, 128), F32),
            V((3, 26, 40, 128), F32),
            V((3, 24, 24, 128), F32),
            V((3, 24, 24, 128), F32),
            V((1536, 512), BF16),
            V((512, 512), BF16),
            V((512, 1536), BF16),
            V((1536, 512), BF16),
            V((1536, 512), BF16),
            V((256, 256), BF16),
            V((1152, 128), F32),
            V((1152, 128), F32),
            V((2, ROWS, WIDE), F32),
            V((2, ROWS, WIDE), BF16),
            V((2, ROWS, WIDE), F32),
            V((2, 32, 128), F32),
            V((2, 32, 128), F32),
            V((8, 128), F32),
            V((16, 8, 128), F32),
            V((2, 2, 3, 24, 128), F32),
            V((2, 2, 3, 24, 128), F32),
            V((512, WIDE), BF16),
            V((8, 128), BF16),
            V((512, 512), F32),
            V((8, 128), F32),
            V((512, 512), BF16),
            V((512, 512), BF16),
            V((512, WIDE), BF16),
            V((512, 512), BF16),
            V((512, 512), BF16),
            V((7168, 128), F32),
            V((3, 16, 2, 24, 128), F32),
            V((3, 8, 4, 24, 128), F32),
            V((7, 16, 8, 128), F32),
            V((16, 2, 24, 128), F32),
            V((8, 4, 24, 128), F32),
            V((2, 4, 2, 8, 128), F32),
            V((3, 8, 24, 128), F32),
            V((3, 8, 24, 128), F32),
            V((3, 2, 2, 8, 128), F32),
            V((8, 48, 128), F32),
            V((2, 2, 8, 128), F32),
            V((7, 48, 128), F32),
            V((3, 8, 128), F32),
            pltpu.SemaphoreType.DMA((6,)),
            pltpu.SemaphoreType.DMA((60,)),
            pltpu.SemaphoreType.DMA((60,)),
        ],
        compiler_params=pltpu.CompilerParams(
            collective_id=0, has_side_effects=True, vmem_limit_bytes=60 * 2**20
        ),
    )(
        velocity, target_field, w_in, w_mid, w_out,
        moment_one.reshape(56, 128), moment_two.reshape(56, 128),
        picks.reshape(1, 32), owners.reshape(1, 32), counts,
    )
    return next_velocity, direction.reshape(7168)


def solution(mesh):
    return jax.shard_map(
        local,
        mesh=mesh,
        in_specs=(
            P(None, "gx", ("role", "gy"), None),
            P(None, "gx", ("role", "gy"), None),
            P(),
            P(),
            P(),
            P(("role", "gx", "gy")),
            P(("role", "gx", "gy")),
            P(("role", "gx", "gy")),
            P(("role", "gx", "gy")),
            P(("role", "gy"), "gx"),
        ),
        out_specs=(P(None, "gx", ("role", "gy"), None), P(("role", "gx", "gy"))),
        check_vma=False,
    )
```

time: 466 us -> 67.2 us (0.14)
  waiting for transfers between devices: 233 us -> 0 us
  local copies, waits for them, and re-layouts: 119 us -> 2.76 us
  Pallas kernels: 0 us -> 62.5 us
  blocking collectives: 40.3 us -> 0 us
  other arithmetic: 20.1 us -> 0 us
  matrix products: 20 us -> 0 us
  starting transfers between devices: 17.1 us -> 0 us
  between operations: 15 us -> 1.3 us
    psum x1 -> x0, waiting for transfers between devices: 233 us -> none  [local(): grad_whole = lax.psum(grad_flat, ('role', 'gx', 'gy'))]
    pallas_call x0 -> x1, Pallas kernels: none -> 62.5 us  [local(): pl.pallas_call(kernel, out_shape=(jax.ShapeDtypeStruct(velocity.shape, F3...]
    transpose x13 -> x0, local copies, waits for them, and re-layouts: 48.7 us -> none  [the longest x1 38.4 us: gradient(): grad_out.reshape(hidden_size, BLOCK, 3, BLOCK, BLOCK)]
    reshape x7 -> x0, local copies, waits for them, and re-layouts: 45 us -> none  [the longest x1 34.9 us: gradient(): grad_out.reshape(-1)]
    psum x1 -> x0, blocking collectives: 40.3 us -> none  [local(): totals = lax.psum(jnp.sum(match.astype(jnp.float32), axis=0), 'gx')]
    dot_general x11 -> x0, matrix products: 20 us -> none  [the longest x2 5.67 us: closure_rows(): return jnp.dot(hidden_two, w_last, preferred_element_type=jnp.float32)]
    ppermute x8 -> x0, starting transfers between devices: 17.1 us -> none  [the longest x4 9.16 us: extended(): before = lax.ppermute(last, axis, up)]
    slice x7 -> x0, local copies, waits for them, and re-layouts: 10.8 us -> none  [the longest x4 7.53 us: tendency(): third_up = jnp.roll(field, -1, 3)]
  transfers between devices with their start and end apart: 9 -> 0, of which waited for: 1 -> 0; matrix products, arithmetic and copies ran while one was open for 33% -> 0% of each run, Pallas kernels for 0% -> 0%
where the time goes in v1:
time: 67.2 us; the launch traced here: 66.6 us
  Pallas kernels  62.5 us (93%)
  local copies, waits for them, and re-layouts  2.76 us (4%)
  between operations  1.3 us (2%)
    pallas_call x1, Pallas kernels, local(): pl.pallas_call(kernel, out_shape=(jax.ShapeDtypeStruct(velocity.shape, F3...  62.5 us
    unnamed x4, local copies, waits for them, and re-layouts  2.76 us

profile of v1, /device:TPU:4, one launch (start us, length us, event | category | flops | bytes accessed | tf_op | source)
XLA Modules:
  0.0 66.6 jit_solution(14798023258263867312)
XLA Ops:
  1.3 62.5 %shard_map.113 = (f32[3,24,24,128]{3,2,1,0:T(8,128)}, f32[56,128]{1,0:T(8,128)}) custom-call(f32[3,24,24,128]{3,2,1,0:T(8,128)} %vel_hbm.1, f32[3,24,24,128]{3,2,1,0:T(8,128)} %tgt_hbm.1, bf16[1536,512]{1,0:T(8,128)(2,1)} %win_hbm.1, bf16[512,512]{1,0:T(8,128)(2,1)} %wmid_hbm.1, bf16[512,1536]{1,0:T(8,128)(2,1)} %wout_hbm.1, f32[56,128]{1,0:T(8,128)} %bitcast.5, ...), custom_call_target="tpu_custom_call" | custom-call | tf_op jit(solution)/shard_map/pallas_call | solution.py:471
  63.8 0.0 copy-start
  63.8 2.1 %copy.15 = f32[3,24,24,128]{3,2,1,0:T(8,128)} copy(f32[3,24,24,128]{3,2,1,0:T(8,128)} %get-tuple-element.8) | data formatting | bytes 1769472
  66.0 0.0 copy-done
  66.0 0.6 copy.16
Async XLA Ops:
  63.8 2.2 %copy-start = (f32[56,128]{1,0:T(8,128)S(1)}, f32[56,128]{1,0:T(8,128)}, u32[]{:S(2)}) copy-start(f32[56,128]{1,0:T(8,128)} %get-tuple-element.5) | copy-start | bytes 86020

commit v2 on v1

--- a/solution.py
+++ b/solution.py
@@ -48,11 +48,12 @@
 
 def kernel(
     vel_hbm, tgt_hbm, win_hbm, wmid_hbm, wout_hbm, mom1, mom2, picks, owners, counts,
-    next_hbm, direction,
-    vp, sp, vnext, tgt, w_in, w_mid, w_out, w_first, w_last, perm,
+    vnext, direction,
+    vp, sp, tgt, w_in, w_mid, w_out, w_first, w_last, perm,
     t_zero, t_one, xf, xb, yf, info, weight, hist_out, hist, ysend, yrecv,
-    xs, ys, slope_one, slope_two, h_one, h_two, e_all, b_two, b_one,
+    xs, slope_one, slope_two, h_one, h_two, e_all, b_two, b_one,
     grad, rx, ry, rz, sx, sy, sz, rx2, ry2, rz2, sxy, sz2, rxy3, rz3,
+    rxs, rys, sxs, syt, rx2s, ry2s, sxys, rxy3s,
     load_sem, send_sem, recv_sem,
 ):
     r = lax.axis_index("role")
@@ -136,11 +137,6 @@
         c.start()
         return c
 
-    pl.semaphore_wait(barrier, 22)
-
-    hist_copies = [send(hist_out, hist.at[i], at_i(i + d)) for d in range(1, 16)]
-    pair_info = send(info.at[0], info.at[1], pair)
-
     def halo_start(field, slot):
         flat = field.reshape(3 * 26 * 40, 128)
         for c in range(3):
@@ -190,6 +186,22 @@
     pr = lax.broadcasted_iota(jnp.int32, (256, 256), 0)
     pc = lax.broadcasted_iota(jnp.int32, (256, 256), 1)
     perm[...] = jnp.where(pc == (pr & 31) * 8 + (pr >> 5), 1.0, 0.0).astype(BF16)
+
+    pl.semaphore_wait(barrier, 22)
+    hist_copies = [send(hist_out, hist.at[i], at_i(i + d)) for d in range(1, 16)]
+    pair_info = send(info.at[0], info.at[1], pair)
+
+    load_v.wait()
+    turn(take_from(vp))
+
+    def write_x(at, tile):
+        xf[0, :, at : at + 128] = tile
+        xb[0, :, at : at + 128] = tile.astype(BF16)
+
+    rows_of(write_x)
+
+    pair_x = send(xf.at[0], xf.at[1], pair)
+    halo_one = halo_start(vp, 0)
 
     load_t.wait()
 
@@ -212,56 +224,30 @@
         yf[0, :, 256 * g : 256 * g + 256] = dot(jnp.concatenate(tiles, axis=1), perm[...])
     pair_y = send(yf.at[0], yf.at[1], pair)
 
-    load_v.wait()
-    halo_one = halo_start(vp, 0)
-    turn(take_from(vp))
-
-    def write_x(at, tile):
-        xf[0, :, at : at + 128] = tile
-        xb[0, :, at : at + 128] = tile.astype(BF16)
-
-    rows_of(write_x)
-    pair_x = send(xf.at[0], xf.at[1], pair)
-
-    for c in hist_copies:
-        c.wait_recv()
-    totals = jnp.sum(hist[...], axis=0)
-    inverse = 1.0 / jnp.maximum(totals, 1.0)
-    own_weight = jnp.sum(match * inverse[0:1, :], axis=1, keepdims=True)
-    weight[0] = jnp.broadcast_to(own_weight, (32, 128))
-    pair_w = send(weight.at[0], weight.at[1], pair)
-
-    load_wi.wait()
-    load_wo.wait()
-    load_wm.wait()
-    for g in range(6):
-        wi = dot(perm[...], w_in[256 * g : 256 * g + 256, :]).astype(BF16)
-        wo = dot(perm[...], w_out[:, 256 * g : 256 * g + 256], NT).astype(BF16)
+    def block_order(g, value, dst):
         for oz in range(8):
             at = oz * 128 + 32 * g if g < 4 else 1024 + oz * 64 + 32 * (g - 4)
-            w_first[at : at + 32, :] = wi[32 * oz : 32 * oz + 32]
-            w_last[at : at + 32, :] = wo[32 * oz : 32 * oz + 32]
-
-    for c in (pair_info, pair_y, pair_x, pair_w):
-        c.wait_recv()
-
-    def side(s, carry):
-        rows = pl.ds(pl.multiple_of(s * 256, 256), 256)
-
-        @pl.when(s == 1)
-        def _():
-            xb[1] = xf[1].astype(BF16)
-
+            dst[at : at + 32, :] = value[32 * oz : 32 * oz + 32].astype(BF16)
+
+    load_wi.wait()
+    for g in range(6):
+        block_order(g, dot(perm[...], w_in[256 * g : 256 * g + 256, :]), w_first)
+
+    def choose(s):
         start = info[s]
         start = jnp.concatenate([start, start], axis=1)[:, :ROWS]
         block = lax.broadcasted_iota(jnp.int32, (32, ROWS), 1).astype(F32)
-        chosen = jnp.concatenate(
+        return jnp.concatenate(
             [
                 jnp.where(block == start + float(k // 4 * 48 + k // 2 % 2 * 16 + k % 2), 1.0, 0.0)
                 for k in range(8)
             ],
             axis=0,
         ).astype(BF16)
+
+    def forward(s):
+        rows = slice(256 * s, 256 * s + 256)
+        chosen = choose(s)
         for n in range(3):
             cols = slice(512 * n, 512 * n + 512)
             xs[rows, cols] = dot(chosen, xb[s, :, cols]).astype(BF16)
@@ -270,63 +256,23 @@
         h1 = a.astype(BF16)
         h_one[rows, :] = h1
         a, slope = gelu_and_slope(dot(h1, w_mid[...]))
-        h2 = a.astype(BF16)
-        h_two[rows, :] = h2
+        slope_two[rows, :] = slope
+        h_two[rows, :] = a.astype(BF16)
+
+    def backward(s):
+        rows = slice(256 * s, 256 * s + 256)
+        chosen = choose(s)
         w8 = 2.0 * jnp.concatenate([weight[s]] * 8, axis=0)
         w8 = jnp.concatenate([w8] * 4, axis=1)
         up = None
         for n in range(3):
             cols = slice(512 * n, 512 * n + 512)
             target = dot(chosen, yf[s, :, cols].astype(BF16))
-            e = (w8 * (dot(h2, w_out[:, cols]) - target)).astype(BF16)
+            e = (w8 * (dot(h_two[rows, :], w_out[:, cols]) - target)).astype(BF16)
             e_all[rows, cols] = e
             part = dot(e, w_out[:, cols], NT)
             up = part if up is None else up + part
-        b_two[rows, :] = (slope * up).astype(BF16)
-        return carry
-
-    lax.fori_loop(0, 2, side, 0)
-
-    def put(value, start, stride, size):
-        for cb in range(value.shape[1] // 128):
-            grad_flat[pl.ds(start + cb, size, stride=stride), :] = value[:, cb * 128 : cb * 128 + 128]
-
-    grad_flat = grad.reshape(7168, 128)
-
-    @pl.when(r == 0)
-    def _():
-        for s in range(2):
-            rows = slice(256 * s, 256 * s + 256)
-            up = dot(b_two[rows, :], w_mid[...], NT)
-            b_one[rows, :] = (slope_one[rows, :] * up).astype(BF16)
-        for k in range(4):
-            part = dot(xs[:, 256 * k : 256 * k + 256], b_one[...], TN)
-            put(part[:128], 8 * k, 32, 128)
-            put(part[128:], 8 * k + 4, 32, 128)
-        for k in range(2):
-            part = dot(xs[:, 1024 + 256 * k : 1280 + 256 * k], b_one[...], TN)
-            for m in range(4):
-                put(part[64 * m : 64 * m + 64], 4096 + 4 * (4 * k + m), 32, 64)
-        put(dot(h_one[:, 0:256], b_two[...], TN), 6144, 4, 256)
-
-    @pl.when(r == 1)
-    def _():
-        for k in range(2):
-            for n in range(3):
-                part = dot(h_two[:, 256 * k : 256 * k + 256], e_all[:, 512 * n : 512 * n + 512], TN)
-                put(part, 1024 + 3072 * k + 4 * n, 12, 256)
-        put(dot(h_one[:, 256:512], b_two[...], TN), 0, 4, 256)
-
-    gx5 = grad.reshape(16, 4, 2, 56, 128)
-    gy6 = grad.reshape(8, 2, 4, 2, 56, 128)
-    gz = grad.reshape(8, 16, 56, 128)
-    copies_x, copies_y, copies_z = [], [], []
-    for d in range(1, 4):
-        copies_x.append(send(gx5.at[:, lax.rem(x + d, 4), :, 0:24, :], rx.at[d - 1], along_x(d)))
-        k = lax.rem(y + d, 4)
-        copies_y.append(send(gy6.at[:, k // 2, :, k % 2, 24:48, :], ry.at[d - 1], along_y(d)))
-    for d in range(1, 8):
-        copies_z.append(send(gz.at[lax.rem(z + d, 8), :, 48:56, :], rz.at[d - 1], along_z(d)))
+        b_two[rows, :] = (slope_two[rows, :] * up).astype(BF16)
 
     def closure(rows):
         q1 = gelu(dot(rows, w_first[...])).astype(BF16)
@@ -375,8 +321,80 @@
 
         lax.fori_loop(0, 9, body, 0)
 
+    load_wm.wait()
+    load_wo.wait()
+    forward(0)
+    pair_info.wait_recv()
+    pair_x.wait_recv()
+    xb[1] = xf[1].astype(BF16)
+    forward(1)
+
+    for c in hist_copies:
+        c.wait_recv()
+    totals = jnp.sum(hist[...], axis=0)
+    inverse = 1.0 / jnp.maximum(totals, 1.0)
+    own_weight = jnp.sum(match * inverse[0:1, :], axis=1, keepdims=True)
+    weight[0] = jnp.broadcast_to(own_weight, (32, 128))
+    pair_w = send(weight.at[0], weight.at[1], pair)
+
+    backward(0)
+    pair_y.wait_recv()
+    pair_w.wait_recv()
+    backward(1)
+
+    def put(value, start, stride, size):
+        for cb in range(value.shape[1] // 128):
+            grad_flat[pl.ds(start + cb, size, stride=stride), :] = value[:, cb * 128 : cb * 128 + 128]
+
+    grad_flat = grad.reshape(7168, 128)
+
+    @pl.when(r == 0)
+    def _():
+        for s in range(2):
+            rows = slice(256 * s, 256 * s + 256)
+            up = dot(b_two[rows, :], w_mid[...], NT)
+            b_one[rows, :] = (slope_one[rows, :] * up).astype(BF16)
+        for k in range(4):
+            part = dot(xs[:, 256 * k : 256 * k + 256], b_one[...], TN)
+            put(part[:128], 8 * k, 32, 128)
+            put(part[128:], 8 * k + 4, 32, 128)
+        for k in range(2):
+            part = dot(xs[:, 1024 + 256 * k : 1280 + 256 * k], b_one[...], TN)
+            for m in range(4):
+                put(part[64 * m : 64 * m + 64], 4096 + 4 * (4 * k + m), 32, 64)
+        put(dot(h_one[:, 0:256], b_two[...], TN), 6144, 4, 256)
+
+    @pl.when(r == 1)
+    def _():
+        for k in range(2):
+            for n in range(3):
+                part = dot(h_two[:, 256 * k : 256 * k + 256], e_all[:, 512 * n : 512 * n + 512], TN)
+                put(part, 1024 + 3072 * k + 4 * n, 12, 256)
+        put(dot(h_one[:, 256:512], b_two[...], TN), 0, 4, 256)
+
+    gx5 = grad.reshape(16, 4, 2, 56, 128)
+    gy6 = grad.reshape(8, 2, 4, 2, 56, 128)
+    gz = grad.reshape(8, 16, 56, 128)
+    copies_z = []
+
+    def first_phase(at, size, from_x, from_y):
+        to_x, to_y = [], []
+        for d in range(1, 4):
+            to_x.append(send(gx5.at[:, lax.rem(x + d, 4), :, at : at + size, :], from_x.at[d - 1], along_x(d)))
+            k = lax.rem(y + d, 4)
+            here = slice(24 + at, 24 + at + size)
+            to_y.append(send(gy6.at[:, k // 2, :, k % 2, here, :], from_y.at[d - 1], along_y(d)))
+        return to_x, to_y
+
+    big_x, big_y = first_phase(0, 16, rx, ry)
+    for d in range(1, 8):
+        copies_z.append(send(gz.at[lax.rem(z + d, 8), :, 48:56, :], rz.at[d - 1], along_z(d)))
+    small_x, small_y = first_phase(16, 8, rxs, rys)
+
+    for g in range(6):
+        block_order(g, dot(perm[...], w_out[:, 256 * g : 256 * g + 256], NT), w_last)
+    closure(xb[0])
     halo_finish(vp, 0, halo_one)
-    closure(xb[0])
 
     def finish_one(c, bx, by, mid, rate):
         here = pl.ds(pl.multiple_of(by * 8 + 8, 8), 8)
@@ -391,6 +409,51 @@
 
     rows_of(write_second)
     closure(xb[1])
+    def second_phase(at, size, to_x, to_y, from_x, from_y, sum_x, sum_y, next_x, next_y):
+        out_x, out_y = [], []
+        for c in to_x:
+            c.wait_recv()
+        for k in range(16):
+            sum_x[k] = gx5[k, x, :, at : at + size, :] + (from_x[0, k] + from_x[1, k] + from_x[2, k])
+        view = sum_x.reshape(8, 2, 2, size, 128)
+        for d in range(1, 4):
+            k = lax.rem(y + d, 4)
+            out_x.append(send(view.at[:, k // 2, k % 2], next_x.at[d - 1], along_y(d)))
+        for c in to_y:
+            c.wait_recv()
+        here = slice(24 + at, 24 + at + size)
+        for k in range(8):
+            sum_y[k] = gy6[k, yh, :, yl, here, :] + (from_y[0, k] + from_y[1, k] + from_y[2, k])
+        for d in range(1, 4):
+            out_y.append(send(sum_y.at[:, lax.rem(x + d, 4)], next_y.at[d - 1], along_x(d)))
+        return out_x, out_y
+
+    def third_phase(size, out_x, out_y, sum_x, sum_y, next_x, next_y, both, arrived):
+        view = sum_x.reshape(8, 2, 2, size, 128)
+        for c in out_x:
+            c.wait_recv()
+        for k in range(8):
+            both[k, 0:size, :] = view[k, yh, yl] + (next_x[0, k] + next_x[1, k] + next_x[2, k])
+        for c in out_y:
+            c.wait_recv()
+        for k in range(8):
+            both[k, size : 2 * size, :] = sum_y[k, x] + (next_y[0, k] + next_y[1, k] + next_y[2, k])
+        return [send(both.at[lax.rem(z + d, 8)], arrived.at[d - 1], along_z(d)) for d in range(1, 8)]
+
+    big_out_x, big_out_y = second_phase(0, 16, big_x, big_y, rx, ry, sx, sy, rx2, ry2)
+    for c in copies_z:
+        c.wait_recv()
+    total = gz[z, :, 48:56, :]
+    for d in range(7):
+        total = total + rz[d]
+    sz[...] = total.reshape(2, 4, 2, 8, 128)
+    next_z = []
+    for d in range(1, 4):
+        next_z.append(send(sz.at[:, lax.rem(x + d, 4)], rz2.at[d - 1], along_x(d)))
+    small_out_x, small_out_y = second_phase(16, 8, small_x, small_y, rxs, rys, sxs, syt, rx2s, ry2s)
+
+    last_big = third_phase(16, big_out_x, big_out_y, sx, sy, rx2, ry2, sxy, rxy3)
+
     halo_finish(sp, 1, halo_two)
 
     def finish_two(c, bx, by, mid, rate):
@@ -401,42 +464,7 @@
         )
 
     section(sp, finish_two)
-    store = pltpu.make_async_copy(vnext, next_hbm, load_sem.at[5])
-    store.start()
-
-    for c in copies_x:
-        c.wait_recv()
-    for k in range(16):
-        sx[k] = gx5[k, x, :, 0:24, :] + (rx[0, k] + rx[1, k] + rx[2, k])
-    sx6 = sx.reshape(8, 2, 2, 24, 128)
-    next_x, next_y, next_z = [], [], []
-    for d in range(1, 4):
-        k = lax.rem(y + d, 4)
-        next_x.append(send(sx6.at[:, k // 2, k % 2], rx2.at[d - 1], along_y(d)))
-    for c in copies_y:
-        c.wait_recv()
-    for k in range(8):
-        sy[k] = gy6[k, yh, :, yl, 24:48, :] + (ry[0, k] + ry[1, k] + ry[2, k])
-    for d in range(1, 4):
-        next_y.append(send(sy.at[:, lax.rem(x + d, 4)], ry2.at[d - 1], along_x(d)))
-    for c in copies_z:
-        c.wait_recv()
-    total = gz[z, :, 48:56, :]
-    for d in range(7):
-        total = total + rz[d]
-    sz[...] = total.reshape(2, 4, 2, 8, 128)
-    for d in range(1, 4):
-        next_z.append(send(sz.at[:, lax.rem(x + d, 4)], rz2.at[d - 1], along_x(d)))
-
-    for c in next_x:
-        c.wait_recv()
-    for k in range(8):
-        sxy[k, 0:24, :] = sx6[k, yh, yl] + (rx2[0, k] + rx2[1, k] + rx2[2, k])
-    for c in next_y:
-        c.wait_recv()
-    for k in range(8):
-        sxy[k, 24:48, :] = sy[k, x] + (ry2[0, k] + ry2[1, k] + ry2[2, k])
-    last = [send(sxy.at[lax.rem(z + d, 8)], rxy3.at[d - 1], along_z(d)) for d in range(1, 8)]
+
     for c in next_z:
         c.wait_recv()
     sz2[...] = sz[:, x] + (rz2[0] + rz2[1] + rz2[2])
@@ -444,13 +472,16 @@
     for d in range(1, 4):
         k = lax.rem(y + d, 4)
         last_z.append(send(sz2.at[k // 2, k % 2], rz3.at[d - 1], along_y(d)))
-    for c in last + last_z:
+    last_small = third_phase(8, small_out_x, small_out_y, sxs, syt, rx2s, ry2s, sxys, rxy3s)
+    for c in last_big + last_z + last_small:
         c.wait_recv()
     front = sxy[z]
+    tail = sxys[z]
     for d in range(7):
         front = front + rxy3[d]
+        tail = tail + rxy3s[d]
     back = sz2[yh, yl] + (rz3[0] + rz3[1] + rz3[2])
-    g = jnp.concatenate([front, back], axis=0)
+    g = jnp.concatenate([front[:16], tail[:8], front[16:], tail[8:], back], axis=0)
     moment = BETA_ONE * mom1[...] + (1.0 - BETA_ONE) * g
     second = BETA_TWO * mom2[...] + (1.0 - BETA_TWO) * g * g
     corrected = moment / (1.0 - BETA_ONE**ADAM_STEP)
@@ -458,10 +489,10 @@
 
     for c in (
         hist_copies + [pair_info, pair_y, pair_x, pair_w] + halo_one + halo_two
-        + copies_x + copies_y + copies_z + next_x + next_y + next_z + last + last_z
+        + big_x + big_y + small_x + small_y + copies_z + big_out_x + big_out_y + small_out_x + small_out_y
+        + next_z + last_big + last_small + last_z
     ):
         c.wait_send()
-    store.wait()
 
 
 def local(velocity, target_field, w_in, w_mid, w_out, moment_one, moment_two, picks, owners, counts):
@@ -471,15 +502,14 @@
     next_velocity, direction = pl.pallas_call(
         kernel,
         out_shape=(
-            jax.ShapeDtypeStruct(velocity.shape, F32),
-            jax.ShapeDtypeStruct((56, 128), F32),
+            pltpu.VMEM(velocity.shape, F32),
+            pltpu.VMEM((56, 128), F32),
         ),
         in_specs=[any_space] * 5 + [vmem] * 5,
-        out_specs=(any_space, vmem),
+        out_specs=(vmem, vmem),
         scratch_shapes=[
             V((3, 26, 40, 128), F32),
             V((3, 26, 40, 128), F32),
-            V((3, 24, 24, 128), F32),
             V((3, 24, 24, 128), F32),
             V((1536, 512), BF16),
             V((512, 512), BF16),
@@ -499,31 +529,38 @@
             V((2, 2, 3, 24, 128), F32),
             V((2, 2, 3, 24, 128), F32),
             V((512, WIDE), BF16),
-            V((8, 128), BF16),
             V((512, 512), F32),
-            V((8, 128), F32),
+            V((512, 512), F32),
             V((512, 512), BF16),
             V((512, 512), BF16),
             V((512, WIDE), BF16),
             V((512, 512), BF16),
             V((512, 512), BF16),
             V((7168, 128), F32),
-            V((3, 16, 2, 24, 128), F32),
-            V((3, 8, 4, 24, 128), F32),
+            V((3, 16, 2, 16, 128), F32),
+            V((3, 8, 4, 16, 128), F32),
             V((7, 16, 8, 128), F32),
-            V((16, 2, 24, 128), F32),
-            V((8, 4, 24, 128), F32),
+            V((16, 2, 16, 128), F32),
+            V((8, 4, 16, 128), F32),
             V((2, 4, 2, 8, 128), F32),
-            V((3, 8, 24, 128), F32),
-            V((3, 8, 24, 128), F32),
+            V((3, 8, 16, 128), F32),
+            V((3, 8, 16, 128), F32),
             V((3, 2, 2, 8, 128), F32),
-            V((8, 48, 128), F32),
+            V((8, 32, 128), F32),
             V((2, 2, 8, 128), F32),
-            V((7, 48, 128), F32),
+            V((7, 32, 128), F32),
             V((3, 8, 128), F32),
-            pltpu.SemaphoreType.DMA((6,)),
-            pltpu.SemaphoreType.DMA((60,)),
-            pltpu.SemaphoreType.DMA((60,)),
+            V((3, 16, 2, 8, 128), F32),
+            V((3, 8, 4, 8, 128), F32),
+            V((16, 2, 8, 128), F32),
+            V((8, 4, 8, 128), F32),
+            V((3, 8, 8, 128), F32),
+            V((3, 8, 8, 128), F32),
+            V((8, 16, 128), F32),
+            V((7, 16, 128), F32),
+            pltpu.SemaphoreType.DMA((5,)),
+            pltpu.SemaphoreType.DMA((80,)),
+            pltpu.SemaphoreType.DMA((80,)),
         ],
         compiler_params=pltpu.CompilerParams(
             collective_id=0, has_side_effects=True, vmem_limit_bytes=60 * 2**20

time: 67.2 us -> 58.8 us (0.87)
  Pallas kernels: 62.5 us -> 55.8 us
  local copies, waits for them, and re-layouts: 2.76 us -> 1.53 us
    pallas_call x1, Pallas kernels: 62.5 us -> 55.8 us  [local(): pl.pallas_call(kernel, out_shape=(pltpu.VMEM(velocity.shape, F32), pltpu....]
    unnamed x4 -> x2, local copies, waits for them, and re-layouts: 2.76 us -> 1.53 us
where the time goes in v2:
time: 58.8 us; the launch traced here: 58.6 us
  Pallas kernels  55.8 us (95%)
  local copies, waits for them, and re-layouts  1.53 us (3%)
  between operations  1.29 us (2%)
    pallas_call x1, Pallas kernels, local(): pl.pallas_call(kernel, out_shape=(pltpu.VMEM(velocity.shape, F32), pltpu....  55.8 us
    unnamed x2, local copies, waits for them, and re-layouts  1.53 us

profile of v2, /device:TPU:4, one launch (start us, length us, event | category | flops | bytes accessed | tf_op | source)
XLA Modules:
  0.0 58.6 jit_solution(16980196796524317823)
XLA Ops:
  1.3 55.8 %shard_map.113 = (f32[3,24,24,128]{3,2,1,0:T(8,128)S(1)}, f32[56,128]{1,0:T(8,128)S(1)}) custom-call(f32[3,24,24,128]{3,2,1,0:T(8,128)} %vel_hbm.1, f32[3,24,24,128]{3,2,1,0:T(8,128)} %tgt_hbm.1, bf16[1536,512]{1,0:T(8,128)(2,1)} %win_hbm.1, bf16[512,512]{1,0:T(8,128)(2,1)} %wmid_hbm.1, bf16[512,1536]{1,0:T(8,128)(2,1)} %wout_hbm.1, f32[56,128]{1,0:T(8,128)} %bitcast.6, ...), custom_call_target="tpu_custom_call" | custom-call | tf_op jit(solution)/shard_map/pallas_call | solution.py:502
  57.1 0.9 %copy.14 = f32[3,24,24,128]{3,2,1,0:T(8,128)} copy(f32[3,24,24,128]{3,2,1,0:T(8,128)S(1)} %get-tuple-element.6) | data formatting | bytes 1769472
  58.0 0.6 %copy.15 = f32[7168]{0:T(1024)} copy(f32[7168]{0:T(1024)S(1)} %bitcast.5) | data formatting | bytes 57344

commit v3 on v2

--- a/solution.py
+++ b/solution.py
@@ -53,7 +53,7 @@
     t_zero, t_one, xf, xb, yf, info, weight, hist_out, hist, ysend, yrecv,
     xs, slope_one, slope_two, h_one, h_two, e_all, b_two, b_one,
     grad, rx, ry, rz, sx, sy, sz, rx2, ry2, rz2, sxy, sz2, rxy3, rz3,
-    rxs, rys, sxs, syt, rx2s, ry2s, sxys, rxy3s,
+    rxs, rys, sxs, syt, rx2s, ry2s, sxys, rxy3s, fx, fy, fxs, fys,
     load_sem, send_sem, recv_sem,
 ):
     r = lax.axis_index("role")
@@ -98,7 +98,7 @@
 
     barrier = pltpu.get_barrier_semaphore()
     other = at_q(q + 2 * yl - 1)
-    for d in range(1, 16):
+    for d in (8, 7, 9, 6, 10, 5, 11, 4, 12, 3, 13, 2, 14, 1, 15):
         pl.semaphore_signal(barrier, inc=1, device_id=at_i(i + d), device_id_type=MESH)
     for d in range(1, 4):
         pl.semaphore_signal(barrier, inc=1, device_id=along_x(d), device_id_type=MESH)
@@ -188,7 +188,7 @@
     perm[...] = jnp.where(pc == (pr & 31) * 8 + (pr >> 5), 1.0, 0.0).astype(BF16)
 
     pl.semaphore_wait(barrier, 22)
-    hist_copies = [send(hist_out, hist.at[i], at_i(i + d)) for d in range(1, 16)]
+    hist_copies = [send(hist_out, hist.at[i], at_i(i + d)) for d in (8, 7, 9, 6, 10, 5, 11, 4, 12, 3, 13, 2, 14, 1, 15)]
     pair_info = send(info.at[0], info.at[1], pair)
 
     load_v.wait()
@@ -377,23 +377,67 @@
     gz = grad.reshape(8, 16, 56, 128)
     copies_z = []
 
-    def first_phase(at, size, from_x, from_y):
-        to_x, to_y = [], []
-        for d in range(1, 4):
-            to_x.append(send(gx5.at[:, lax.rem(x + d, 4), :, at : at + size, :], from_x.at[d - 1], along_x(d)))
-            k = lax.rem(y + d, 4)
-            here = slice(24 + at, 24 + at + size)
-            to_y.append(send(gy6.at[:, k // 2, :, k % 2, here, :], from_y.at[d - 1], along_y(d)))
-        return to_x, to_y
-
-    big_x, big_y = first_phase(0, 16, rx, ry)
-    for d in range(1, 8):
+    up_x, low_x, up_y, low_y = lax.rem(x + 1, 4), lax.rem(x + 3, 4), lax.rem(y + 1, 4), lax.rem(y + 3, 4)
+
+    def for_x(to, part, rows):
+        return gx5.at[8 * part : 8 * part + 8, to, :, rows, :]
+
+    def for_y(to, part, rows):
+        return gy6.at[4 * part : 4 * part + 4, to // 2, :, to % 2, rows, :]
+
+    def far_phase(at, size, far_x, far_y):
+        rx_rows, ry_rows = slice(at, at + size), slice(24 + at, 24 + at + size)
+        two_x, two_y = lax.rem(x + 2, 4), lax.rem(y + 2, 4)
+        return (
+            [
+                send(for_x(two_x, 0, rx_rows), far_x.at[0], along_x(1)),
+                send(for_x(two_x, 1, rx_rows), far_x.at[1], along_x(3)),
+            ],
+            [
+                send(for_y(two_y, 0, ry_rows), far_y.at[0], along_y(1)),
+                send(for_y(two_y, 1, ry_rows), far_y.at[1], along_y(3)),
+            ],
+        )
+
+    def near_phase(at, size, from_x, from_y):
+        rx_rows, ry_rows = slice(at, at + size), slice(24 + at, 24 + at + size)
+        return (
+            [
+                send(for_x(up_x, 1, rx_rows), from_x.at[0, 1], along_x(1)),
+                send(for_x(low_x, 0, rx_rows), from_x.at[1, 0], along_x(3)),
+            ],
+            [
+                send(for_y(up_y, 1, ry_rows), from_y.at[0, 1], along_y(1)),
+                send(for_y(low_y, 0, ry_rows), from_y.at[1, 0], along_y(3)),
+            ],
+        )
+
+    def merge(at, size, far, near, far_x, far_y, from_x, from_y):
+        rx_rows, ry_rows = slice(at, at + size), slice(24 + at, 24 + at + size)
+        for part, to, way in ((0, up_x, 1), (1, low_x, 3)):
+            far[0][part].wait_recv()
+            for k in range(8):
+                gx5[8 * part + k, to, :, rx_rows, :] = gx5[8 * part + k, to, :, rx_rows, :] + far_x[part, k]
+            near[0].append(send(for_x(to, part, rx_rows), from_x.at[part, part], along_x(way)))
+        for part, to, way in ((0, up_y, 1), (1, low_y, 3)):
+            far[1][part].wait_recv()
+            for k in range(4):
+                there = (4 * part + k, to // 2, slice(None), to % 2, ry_rows, slice(None))
+                gy6[there] = gy6[there] + far_y[part, k]
+            near[1].append(send(for_y(to, part, ry_rows), from_y.at[part, part], along_y(way)))
+
+    big_far = far_phase(0, 16, fx, fy)
+    big_near = near_phase(0, 16, rx, ry)
+    small_far = far_phase(16, 8, fxs, fys)
+    for d in (4, 3, 5, 2, 6, 1, 7):
         copies_z.append(send(gz.at[lax.rem(z + d, 8), :, 48:56, :], rz.at[d - 1], along_z(d)))
-    small_x, small_y = first_phase(16, 8, rxs, rys)
+    merge(0, 16, big_far, big_near, fx, fy, rx, ry)
+    small_near = near_phase(16, 8, rxs, rys)
 
     for g in range(6):
         block_order(g, dot(perm[...], w_out[:, 256 * g : 256 * g + 256], NT), w_last)
     closure(xb[0])
+    merge(16, 8, small_far, small_near, fxs, fys, rxs, rys)
     halo_finish(vp, 0, halo_one)
 
     def finish_one(c, bx, by, mid, rate):
@@ -414,7 +458,7 @@
         for c in to_x:
             c.wait_recv()
         for k in range(16):
-            sum_x[k] = gx5[k, x, :, at : at + size, :] + (from_x[0, k] + from_x[1, k] + from_x[2, k])
+            sum_x[k] = gx5[k, x, :, at : at + size, :] + (from_x[0, k // 8, k % 8] + from_x[1, k // 8, k % 8])
         view = sum_x.reshape(8, 2, 2, size, 128)
         for d in range(1, 4):
             k = lax.rem(y + d, 4)
@@ -423,7 +467,7 @@
             c.wait_recv()
         here = slice(24 + at, 24 + at + size)
         for k in range(8):
-            sum_y[k] = gy6[k, yh, :, yl, here, :] + (from_y[0, k] + from_y[1, k] + from_y[2, k])
+            sum_y[k] = gy6[k, yh, :, yl, here, :] + (from_y[0, k // 4, k % 4] + from_y[1, k // 4, k % 4])
         for d in range(1, 4):
             out_y.append(send(sum_y.at[:, lax.rem(x + d, 4)], next_y.at[d - 1], along_x(d)))
         return out_x, out_y
@@ -438,9 +482,9 @@
             c.wait_recv()
         for k in range(8):
             both[k, size : 2 * size, :] = sum_y[k, x] + (next_y[0, k] + next_y[1, k] + next_y[2, k])
-        return [send(both.at[lax.rem(z + d, 8)], arrived.at[d - 1], along_z(d)) for d in range(1, 8)]
-
-    big_out_x, big_out_y = second_phase(0, 16, big_x, big_y, rx, ry, sx, sy, rx2, ry2)
+        return [send(both.at[lax.rem(z + d, 8)], arrived.at[d - 1], along_z(d)) for d in (4, 3, 5, 2, 6, 1, 7)]
+
+    big_out_x, big_out_y = second_phase(0, 16, big_near[0], big_near[1], rx, ry, sx, sy, rx2, ry2)
     for c in copies_z:
         c.wait_recv()
     total = gz[z, :, 48:56, :]
@@ -450,7 +494,7 @@
     next_z = []
     for d in range(1, 4):
         next_z.append(send(sz.at[:, lax.rem(x + d, 4)], rz2.at[d - 1], along_x(d)))
-    small_out_x, small_out_y = second_phase(16, 8, small_x, small_y, rxs, rys, sxs, syt, rx2s, ry2s)
+    small_out_x, small_out_y = second_phase(16, 8, small_near[0], small_near[1], rxs, rys, sxs, syt, rx2s, ry2s)
 
     last_big = third_phase(16, big_out_x, big_out_y, sx, sy, rx2, ry2, sxy, rxy3)
 
@@ -489,7 +533,8 @@
 
     for c in (
         hist_copies + [pair_info, pair_y, pair_x, pair_w] + halo_one + halo_two
-        + big_x + big_y + small_x + small_y + copies_z + big_out_x + big_out_y + small_out_x + small_out_y
+        + big_far[0] + big_far[1] + big_near[0] + big_near[1] + small_far[0] + small_far[1]
+        + small_near[0] + small_near[1] + copies_z + big_out_x + big_out_y + small_out_x + small_out_y
         + next_z + last_big + last_small + last_z
     ):
         c.wait_send()
@@ -537,8 +582,8 @@
             V((512, 512), BF16),
             V((512, 512), BF16),
             V((7168, 128), F32),
-            V((3, 16, 2, 16, 128), F32),
-            V((3, 8, 4, 16, 128), F32),
+            V((2, 2, 8, 2, 16, 128), F32),
+            V((2, 2, 4, 4, 16, 128), F32),
             V((7, 16, 8, 128), F32),
             V((16, 2, 16, 128), F32),
             V((8, 4, 16, 128), F32),
@@ -550,17 +595,21 @@
             V((2, 2, 8, 128), F32),
             V((7, 32, 128), F32),
             V((3, 8, 128), F32),
-            V((3, 16, 2, 8, 128), F32),
-            V((3, 8, 4, 8, 128), F32),
+            V((2, 2, 8, 2, 8, 128), F32),
+            V((2, 2, 4, 4, 8, 128), F32),
             V((16, 2, 8, 128), F32),
             V((8, 4, 8, 128), F32),
             V((3, 8, 8, 128), F32),
             V((3, 8, 8, 128), F32),
             V((8, 16, 128), F32),
             V((7, 16, 128), F32),
+            V((2, 8, 2, 16, 128), F32),
+            V((2, 4, 4, 16, 128), F32),
+            V((2, 8, 2, 8, 128), F32),
+            V((2, 4, 4, 8, 128), F32),
             pltpu.SemaphoreType.DMA((5,)),
-            pltpu.SemaphoreType.DMA((80,)),
-            pltpu.SemaphoreType.DMA((80,)),
+            pltpu.SemaphoreType.DMA((90,)),
+            pltpu.SemaphoreType.DMA((90,)),
         ],
         compiler_params=pltpu.CompilerParams(
             collective_id=0, has_side_effects=True, vmem_limit_bytes=60 * 2**20

time: 58.8 us -> 54 us (0.918)
  Pallas kernels: 55.8 us -> 51.1 us
    pallas_call x1, Pallas kernels: 55.8 us -> 51.1 us  [local(): pl.pallas_call(kernel, out_shape=(pltpu.VMEM(velocity.shape, F32), pltpu....]
where the time goes in v3:
time: 54 us; the launch traced here: 53.9 us
  Pallas kernels  51.1 us (95%)
  local copies, waits for them, and re-layouts  1.53 us (3%)
  between operations  1.29 us (2%)
    pallas_call x1, Pallas kernels, local(): pl.pallas_call(kernel, out_shape=(pltpu.VMEM(velocity.shape, F32), pltpu....  51.1 us
    unnamed x2, local copies, waits for them, and re-layouts  1.53 us

profile of v3, /device:TPU:4, one launch (start us, length us, event | category | flops | bytes accessed | tf_op | source)
XLA Modules:
  0.0 53.9 jit_solution(12416944385617786031)
XLA Ops:
  1.3 51.1 %shard_map.113 = (f32[3,24,24,128]{3,2,1,0:T(8,128)S(1)}, f32[56,128]{1,0:T(8,128)S(1)}) custom-call(f32[3,24,24,128]{3,2,1,0:T(8,128)} %vel_hbm.1, f32[3,24,24,128]{3,2,1,0:T(8,128)} %tgt_hbm.1, bf16[1536,512]{1,0:T(8,128)(2,1)} %win_hbm.1, bf16[512,512]{1,0:T(8,128)(2,1)} %wmid_hbm.1, bf16[512,1536]{1,0:T(8,128)(2,1)} %wout_hbm.1, f32[56,128]{1,0:T(8,128)} %bitcast.6, ...), custom_call_target="tpu_custom_call" | custom-call | tf_op jit(solution)/shard_map/pallas_call | solution.py:547
  52.4 0.9 %copy.14 = f32[3,24,24,128]{3,2,1,0:T(8,128)} copy(f32[3,24,24,128]{3,2,1,0:T(8,128)S(1)} %get-tuple-element.6) | data formatting | bytes 1769472
  53.3 0.6 %copy.15 = f32[7168]{0:T(1024)} copy(f32[7168]{0:T(1024)S(1)} %bitcast.5) | data formatting | bytes 57344

commit v4 on v3

--- a/solution.py
+++ b/solution.py
@@ -348,6 +348,11 @@
 
     grad_flat = grad.reshape(7168, 128)
 
+    def out_terms(k):
+        for n in range(3):
+            part = dot(h_two[:, 256 * k : 256 * k + 256], e_all[:, 512 * n : 512 * n + 512], TN)
+            put(part, 1024 + 3072 * k + 4 * n, 12, 256)
+
     @pl.when(r == 0)
     def _():
         for s in range(2):
@@ -358,19 +363,11 @@
             part = dot(xs[:, 256 * k : 256 * k + 256], b_one[...], TN)
             put(part[:128], 8 * k, 32, 128)
             put(part[128:], 8 * k + 4, 32, 128)
-        for k in range(2):
-            part = dot(xs[:, 1024 + 256 * k : 1280 + 256 * k], b_one[...], TN)
-            for m in range(4):
-                put(part[64 * m : 64 * m + 64], 4096 + 4 * (4 * k + m), 32, 64)
-        put(dot(h_one[:, 0:256], b_two[...], TN), 6144, 4, 256)
 
     @pl.when(r == 1)
     def _():
-        for k in range(2):
-            for n in range(3):
-                part = dot(h_two[:, 256 * k : 256 * k + 256], e_all[:, 512 * n : 512 * n + 512], TN)
-                put(part, 1024 + 3072 * k + 4 * n, 12, 256)
         put(dot(h_one[:, 256:512], b_two[...], TN), 0, 4, 256)
+        out_terms(0)
 
     gx5 = grad.reshape(16, 4, 2, 56, 128)
     gy6 = grad.reshape(8, 2, 4, 2, 56, 128)
@@ -385,19 +382,18 @@
     def for_y(to, part, rows):
         return gy6.at[4 * part : 4 * part + 4, to // 2, :, to % 2, rows, :]
 
-    def far_phase(at, size, far_x, far_y):
+    def far_part(part, at, size, far_x, far_y):
         rx_rows, ry_rows = slice(at, at + size), slice(24 + at, 24 + at + size)
         two_x, two_y = lax.rem(x + 2, 4), lax.rem(y + 2, 4)
+        way = 1 + 2 * part
         return (
-            [
-                send(for_x(two_x, 0, rx_rows), far_x.at[0], along_x(1)),
-                send(for_x(two_x, 1, rx_rows), far_x.at[1], along_x(3)),
-            ],
-            [
-                send(for_y(two_y, 0, ry_rows), far_y.at[0], along_y(1)),
-                send(for_y(two_y, 1, ry_rows), far_y.at[1], along_y(3)),
-            ],
+            send(for_x(two_x, part, rx_rows), far_x.at[part], along_x(way)),
+            send(for_y(two_y, part, ry_rows), far_y.at[part], along_y(way)),
         )
+
+    def far_phase(at, size, far_x, far_y):
+        parts = [far_part(part, at, size, far_x, far_y) for part in range(2)]
+        return [c[0] for c in parts], [c[1] for c in parts]
 
     def near_phase(at, size, from_x, from_y):
         rx_rows, ry_rows = slice(at, at + size), slice(24 + at, 24 + at + size)
@@ -426,7 +422,21 @@
                 gy6[there] = gy6[there] + far_y[part, k]
             near[1].append(send(for_y(to, part, ry_rows), from_y.at[part, part], along_y(way)))
 
-    big_far = far_phase(0, 16, fx, fy)
+    early = far_part(0, 0, 16, fx, fy)
+    @pl.when(r == 0)
+    def _():
+        for k in range(2):
+            part = dot(xs[:, 1024 + 256 * k : 1280 + 256 * k], b_one[...], TN)
+            for m in range(4):
+                put(part[64 * m : 64 * m + 64], 4096 + 4 * (4 * k + m), 32, 64)
+        put(dot(h_one[:, 0:256], b_two[...], TN), 6144, 4, 256)
+
+    @pl.when(r == 1)
+    def _():
+        out_terms(1)
+
+    late = far_part(1, 0, 16, fx, fy)
+    big_far = [early[0], late[0]], [early[1], late[1]]
     big_near = near_phase(0, 16, rx, ry)
     small_far = far_phase(16, 8, fxs, fys)
     for d in (4, 3, 5, 2, 6, 1, 7):

time: 54 us -> 53.6 us (level)
  Pallas kernels: 51.1 us -> 50.5 us
    pallas_call x1, Pallas kernels: 51.1 us -> 50.5 us  [local(): pl.pallas_call(kernel, out_shape=(pltpu.VMEM(velocity.shape, F32), pltpu....]
where the time goes in v4:
time: 53.6 us; the launch traced here: 53.3 us
  Pallas kernels  50.5 us (94%)
  local copies, waits for them, and re-layouts  1.53 us (3%)
  between operations  1.29 us (2%)
    pallas_call x1, Pallas kernels, local(): pl.pallas_call(kernel, out_shape=(pltpu.VMEM(velocity.shape, F32), pltpu....  50.5 us
    unnamed x2, local copies, waits for them, and re-layouts  1.53 us

profile of v4, /device:TPU:4, one launch (start us, length us, event | category | flops | bytes accessed | tf_op | source)
XLA Modules:
  0.0 53.3 jit_solution(10880395606521761176)
XLA Ops:
  1.3 50.5 %shard_map.113 = (f32[3,24,24,128]{3,2,1,0:T(8,128)S(1)}, f32[56,128]{1,0:T(8,128)S(1)}) custom-call(f32[3,24,24,128]{3,2,1,0:T(8,128)} %vel_hbm.1, f32[3,24,24,128]{3,2,1,0:T(8,128)} %tgt_hbm.1, bf16[1536,512]{1,0:T(8,128)(2,1)} %win_hbm.1, bf16[512,512]{1,0:T(8,128)(2,1)} %wmid_hbm.1, bf16[512,1536]{1,0:T(8,128)(2,1)} %wout_hbm.1, f32[56,128]{1,0:T(8,128)} %bitcast.6, ...), custom_call_target="tpu_custom_call" | custom-call | tf_op jit(solution)/shard_map/pallas_call | solution.py:557
  51.7 0.9 %copy.14 = f32[3,24,24,128]{3,2,1,0:T(8,128)} copy(f32[3,24,24,128]{3,2,1,0:T(8,128)S(1)} %get-tuple-element.6) | data formatting | bytes 1769472
  52.7 0.6 %copy.15 = f32[7168]{0:T(1024)} copy(f32[7168]{0:T(1024)S(1)} %bitcast.5) | data formatting | bytes 57344

commit v5 on v4

--- a/solution.py
+++ b/solution.py
@@ -53,7 +53,7 @@
     t_zero, t_one, xf, xb, yf, info, weight, hist_out, hist, ysend, yrecv,
     xs, slope_one, slope_two, h_one, h_two, e_all, b_two, b_one,
     grad, rx, ry, rz, sx, sy, sz, rx2, ry2, rz2, sxy, sz2, rxy3, rz3,
-    rxs, rys, sxs, syt, rx2s, ry2s, sxys, rxy3s, fx, fy, fxs, fys,
+    rxs, rys, sxs, syt, rx2s, ry2s, sxys, rxy3s, fx, fy, fxs, fys, miss,
     load_sem, send_sem, recv_sem,
 ):
     r = lax.axis_index("role")
@@ -259,16 +259,22 @@
         slope_two[rows, :] = slope
         h_two[rows, :] = a.astype(BF16)
 
+    def compare(s):
+        rows = slice(256 * s, 256 * s + 256)
+        chosen = choose(s)
+        for n in range(3):
+            cols = slice(512 * n, 512 * n + 512)
+            target = dot(chosen, yf[s, :, cols].astype(BF16))
+            miss[rows, cols] = dot(h_two[rows, :], w_out[:, cols]) - target
+
     def backward(s):
         rows = slice(256 * s, 256 * s + 256)
-        chosen = choose(s)
         w8 = 2.0 * jnp.concatenate([weight[s]] * 8, axis=0)
         w8 = jnp.concatenate([w8] * 4, axis=1)
         up = None
         for n in range(3):
             cols = slice(512 * n, 512 * n + 512)
-            target = dot(chosen, yf[s, :, cols].astype(BF16))
-            e = (w8 * (dot(h_two[rows, :], w_out[:, cols]) - target)).astype(BF16)
+            e = (w8 * miss[rows, cols]).astype(BF16)
             e_all[rows, cols] = e
             part = dot(e, w_out[:, cols], NT)
             up = part if up is None else up + part
@@ -324,6 +330,7 @@
     load_wm.wait()
     load_wo.wait()
     forward(0)
+    compare(0)
     pair_info.wait_recv()
     pair_x.wait_recv()
     xb[1] = xf[1].astype(BF16)
@@ -339,6 +346,7 @@
 
     backward(0)
     pair_y.wait_recv()
+    compare(1)
     pair_w.wait_recv()
     backward(1)
 
@@ -617,6 +625,7 @@
             V((2, 4, 4, 16, 128), F32),
             V((2, 8, 2, 8, 128), F32),
             V((2, 4, 4, 8, 128), F32),
+            V((512, WIDE), F32),
             pltpu.SemaphoreType.DMA((5,)),
             pltpu.SemaphoreType.DMA((90,)),
             pltpu.SemaphoreType.DMA((90,)),

time: 53.6 us -> 53 us (0.989)
  Pallas kernels: 50.5 us -> 49.8 us
    pallas_call x1, Pallas kernels: 50.5 us -> 49.8 us  [local(): pl.pallas_call(kernel, out_shape=(pltpu.VMEM(velocity.shape, F32), pltpu....]
where the time goes in v5:
time: 53 us; the launch traced here: 52.6 us
  Pallas kernels  49.8 us (94%)
  local copies, waits for them, and re-layouts  1.53 us (3%)
  between operations  1.29 us (2%)
    pallas_call x1, Pallas kernels, local(): pl.pallas_call(kernel, out_shape=(pltpu.VMEM(velocity.shape, F32), pltpu....  49.8 us
    unnamed x2, local copies, waits for them, and re-layouts  1.53 us

profile of v5, /device:TPU:4, one launch (start us, length us, event | category | flops | bytes accessed | tf_op | source)
XLA Modules:
  0.0 52.6 jit_solution(4716314881910286029)
XLA Ops:
  1.3 49.8 %shard_map.113 = (f32[3,24,24,128]{3,2,1,0:T(8,128)S(1)}, f32[56,128]{1,0:T(8,128)S(1)}) custom-call(f32[3,24,24,128]{3,2,1,0:T(8,128)} %vel_hbm.1, f32[3,24,24,128]{3,2,1,0:T(8,128)} %tgt_hbm.1, bf16[1536,512]{1,0:T(8,128)(2,1)} %win_hbm.1, bf16[512,512]{1,0:T(8,128)(2,1)} %wmid_hbm.1, bf16[512,1536]{1,0:T(8,128)(2,1)} %wout_hbm.1, f32[56,128]{1,0:T(8,128)} %bitcast.6, ...), custom_call_target="tpu_custom_call" | custom-call | tf_op jit(solution)/shard_map/pallas_call | solution.py:565
  51.1 0.9 %copy.14 = f32[3,24,24,128]{3,2,1,0:T(8,128)} copy(f32[3,24,24,128]{3,2,1,0:T(8,128)S(1)} %get-tuple-element.6) | data formatting | bytes 1769472
  52.0 0.6 %copy.15 = f32[7168]{0:T(1024)} copy(f32[7168]{0:T(1024)S(1)} %bitcast.5) | data formatting | bytes 57344
